TPU v7x, 256 devices: a whole 4x4x8 slice. The times are simulated.
256 devices in a mesh: wide: 64 (over x, z, core), narrow: 4 (over y).
Axes of the slice: x: 4, y: 4, z: 8, core: 2. Of those that a mesh axis runs over, the one named last changes fastest.
Arguments:
- features: bfloat16 [262144, 256], P(('wide', 'narrow')), may hold values from -6 to 6
- cotangent: bfloat16 [262144, 256], P(('wide', 'narrow')), may hold values from -0.059814453 to 0.059814453
- self_weight: bfloat16 [256, 256], replicated, may hold values from -0.375 to 0.375
- bases: bfloat16 [32, 256, 256], replicated, may hold values from -0.375 to 0.375
- basis_coef: bfloat16 [128, 32], P('wide'), may hold values from -1 to 1
- block_values: bfloat16 [128, 256, 128, 128], P('wide', 'narrow'), may hold values from -0.125 to 0.125
- block_slots: int32 [128, 256, 2], P('wide', 'narrow'), may hold values from 0 to 63
- fetch_ids: int32 [16384], P(('wide', 'narrow')), may hold values from 0 to 7
Outputs:
- output: bfloat16 [262144, 256], P(('wide', 'narrow'))
- basis_grad: float32 [8192, 256], P(('wide', 'narrow'))
- coef_grad: float32 [128, 32], P('wide')
All inputs are finite; a program needn't handle non-finite values.
Results may differ from a plain program's by a relative error of at most 0.0056.
Values may be sent and summed in bfloat16 or wider, within the bound.
A program may use at most 128 MiB of HBM per device.

v0:
```python
import jax
import jax.numpy as jnp
from jax import lax
from jax.sharding import PartitionSpec as P


def per_device(
    features, cotangent, self_weight, bases, basis_coef, block_values, block_slots, fetch_ids
):
    wide_count = lax.axis_size("wide")
    block = block_values.shape[2]
    width = features.shape[1]
    fetch = fetch_ids.shape[0]
    per_peer = fetch // wide_count
    owned = features.shape[0] // block
    wanted = fetch_ids.reshape(wide_count, per_peer)
    asked = lax.all_to_all(wanted, "wide", split_axis=0, concat_axis=0, tiled=True)
    asked_flat = asked.reshape(fetch)
    feat_blocks = features.reshape(owned, block, width)
    cot_blocks = cotangent.reshape(owned, block, width)
    send_feat = jnp.take(feat_blocks, asked_flat, axis=0)
    send_cot = jnp.take(cot_blocks, asked_flat, axis=0)
    fetched_feat, fetched_cot = (
        lax.all_to_all(send_feat, "wide", split_axis=0, concat_axis=0, tiled=True),
        lax.all_to_all(send_cot, "wide", split_axis=0, concat_axis=0, tiled=True),
    )
    rel_weights = jnp.einsum(
        "rb,bde->rde", basis_coef, bases, preferred_element_type=jnp.float32
    ).astype(jnp.bfloat16)
    row_slot = block_slots[:, :, 0]
    col_slot = block_slots[:, :, 1]
    col_feat = jnp.take(fetched_feat, col_slot, axis=0)
    gathered = jnp.einsum(
        "rkij,rkjd->rkid", block_values, col_feat, preferred_element_type=jnp.float32
    ).astype(jnp.bfloat16)
    slot_pick = (row_slot[:, :, None] == jnp.arange(fetch, dtype=jnp.int32)[None, None, :]).astype(
        jnp.bfloat16
    )
    slot_gathered = jnp.einsum(
        "rks,rkid->rsid", slot_pick, gathered, preferred_element_type=jnp.float32
    ).astype(jnp.bfloat16)
    slot_sums = jnp.einsum(
        "rsid,rde->sie", slot_gathered, rel_weights, preferred_element_type=jnp.float32
    ).astype(jnp.bfloat16)
    returned = lax.all_to_all(slot_sums, "wide", split_axis=0, concat_axis=0, tiled=True)
    owner_pick = (asked_flat[:, None] == jnp.arange(owned, dtype=jnp.int32)[None, :]).astype(
        jnp.bfloat16
    )
    incoming = jnp.einsum("so,sie->oie", owner_pick, returned, preferred_element_type=jnp.float32)
    self_term = jnp.dot(features, self_weight, preferred_element_type=jnp.float32)
    output = (self_term + incoming.reshape(-1, width)).astype(jnp.bfloat16)
    row_cot = jnp.take(fetched_cot, row_slot, axis=0)
    rel_grads = jnp.einsum("rkid,rkie->rde", gathered, row_cot, preferred_element_type=jnp.float32)
    coef_wide = basis_coef.astype(jnp.float32)
    basis_part = jnp.einsum(
        "rb,rde->bde", coef_wide, rel_grads, precision=lax.Precision.HIGHEST
    ).reshape(-1, width)
    basis_grad = lax.psum_scatter(basis_part, ("wide", "narrow"), scatter_dimension=0, tiled=True)
    coef_part = jnp.einsum(
        "rde,bde->rb",
        rel_grads,
        bases,
        precision=lax.Precision.HIGHEST,
        preferred_element_type=jnp.float32,
    )
    coef_grad = lax.psum(coef_part, "narrow")
    return (output, basis_grad, coef_grad)


def solution(mesh):
    return jax.shard_map(
        per_device,
        mesh=mesh,
        in_specs=(
            P(("wide", "narrow"), None),
            P(("wide", "narrow"), None),
            P(),
            P(),
            P("wide", None),
            P("wide", "narrow", None, None),
            P("wide", "narrow", None),
            P(("wide", "narrow")),
        ),
        out_specs=(P(("wide", "narrow"), None), P(("wide", "narrow"), None), P("wide", None)),
        check_vma=False,
    )
```

profile of v0, /device:TPU:1, one launch (start us, length us, event | category | flops | bytes accessed | tf_op | source)
XLA Modules:
  0.0 1568.2 jit_solution(12343337764896041077)
XLA Ops:
  7.2 0.0 copy-start
  7.2 0.8 copy.35
  8.0 22.1 %all_to_all.24 = s32[64,1,1]{2,1,0:T(1,128)S(1)} all-to-all(s32[64,1,1]{2,1,0:T(1,128)S(1)} %copy.35), channel_id=1, replica_groups=mesh['wide'=64,'narrow'=4] {'wide'}, dimensions={0} | all-to-all | bytes 512 | tf_op jit(solution)/shard_map/all_to_all | solution.py:17
  30.0 1.2 reduce
  31.3 3.8 gather_fusion.2
  35.1 0.0 copy-done
  35.1 2.8 gather_fusion
  37.9 5.2 broadcast_select_fusion
  43.1 100.9 %all_to_all.25 = bf16[64,128,256]{2,1,0:T(8,128)(2,1)} all-to-all(bf16[64,128,256]{2,1,0:T(8,128)(2,1)S(1)} %get-tuple-element.8), channel_id=1, replica_groups=mesh['wide'=64,'narrow'=4] {'wide'}, dimensions={0} | all-to-all | bytes 8388608 | tf_op jit(solution)/shard_map/all_to_all | solution.py:24
  144.0 0.0 copy-start.3
  144.0 6.1 all-to-all-start.3
  150.2 0.2 reduce-scatter.2.cloned.1.call-start
  150.4 0.0 copy-done.3
  150.4 0.1 reshape.79
  150.5 0.1 reshape.85
  150.7 8.8 gather_fusion.1
  159.4 12.0 copy.36
  171.4 11.7 convert_bitcast_fusion
  183.0 63.0 %all-to-all-done.3 = bf16[64,128,256]{2,1,0:T(8,128)(2,1)} async-done(((bf16[64,128,256]{2,1,0:T(8,128)(2,1)}), bf16[64,128,256]{2,1,0:T(8,128)(2,1)}, u32[]{:S(2)}, u32[]{:S(2)}) %all-to-all-start.3) | async-done | bytes 4194336 | tf_op jit(solution)/shard_map/all_to_all | solution.py:25
  246.1 8.8 gather_fusion.3
  254.8 0.0 copy-start.2
  254.8 9.7 fusion.23
  264.6 0.0 copy-done.2
  264.6 3.5 convolution_bitcast_fusion
  268.1 8.1 copy.44
  276.2 0.0 reduce-scatter.2.cloned.1.call-update
  276.2 4.6 fusion.29
  280.8 12.3 copy.37
  293.1 8.3 bitcast_convert_fusion
  301.4 6.5 copy.40
  307.9 5.9 all-to-all-start.2
  313.8 7.9 fusion.32
  321.7 0.0 copy-start.1
  321.7 10.2 psum.7
  332.0 78.0 %all-to-all-done.2 = bf16[64,128,256]{2,1,0:T(8,128)(2,1)} async-done(((bf16[64,128,256]{2,1,0:T(8,128)(2,1)}), bf16[64,128,256]{2,1,0:T(8,128)(2,1)}, u32[]{:S(2)}, u32[]{:S(2)}) %all-to-all-start.2) | async-done | bytes 4194336 | tf_op jit(solution)/shard_map/all_to_all | solution.py:45
  410.0 4.5 fusion.12
  414.5 0.3 copy.42
  414.9 0.0 copy-done.1
  414.9 1.1 fusion.22
  416.0 1145.4 %reduce-scatter.2.cloned.1.call-done = f32[32,256]{1,0:T(8,128)} async-done(((f32[8192,256]{1,0:T(8,128)}), f32[32,256]{1,0:T(8,128)}) %reduce-scatter.2.cloned.1.call-update) | async-done | bytes 32784 | tf_op jit(solution)/shard_map/reduce_scatter | solution.py:58
  (10 shorter events, 0.1 us)
Async XLA Ops:
  7.2 27.9 %copy-start = (bf16[1024,256]{1,0:T(8,128)(2,1)S(1)}, bf16[1024,256]{1,0:T(8,128)(2,1)}, u32[]{:S(2)}) copy-start(bf16[1024,256]{1,0:T(8,128)(2,1)} %param.12) | copy-start | bytes 1572868
  144.0 6.4 copy-start.3
  144.0 102.0 %all-to-all-start.3 = ((bf16[64,128,256]{2,1,0:T(8,128)(2,1)}), bf16[64,128,256]{2,1,0:T(8,128)(2,1)}, u32[]{:S(2)}, u32[]{:S(2)}) async-start(bf16[64,128,256]{2,1,0:T(8,128)(2,1)} %get-tuple-element.7), calls=%async_computation.3 | async-start | bytes 8388608 | tf_op jit(solution)/shard_map/all_to_all | solution.py:25
  150.2 1411.2 %reduce-scatter.2.cloned.1.call-start = ((), (), s32[]{:S(2)}) async-start(), calls=%async_computation.5 | async-start | bytes 8421376 | tf_op jit(solution)/shard_map/reduce_scatter | solution.py:58
  254.8 9.8 copy-start.2
  307.9 102.1 %all-to-all-start.2 = ((bf16[64,128,256]{2,1,0:T(8,128)(2,1)}), bf16[64,128,256]{2,1,0:T(8,128)(2,1)}, u32[]{:S(2)}, u32[]{:S(2)}) async-start(bf16[64,128,256]{2,1,0:T(8,128)(2,1)} %copy.40), calls=%async_computation.2 | async-start | bytes 8388608 | tf_op jit(solution)/shard_map/all_to_all | solution.py:45
  321.7 93.1 %copy-start.1 = (bf16[256,256]{1,0:T(8,128)(2,1)S(1)}, bf16[256,256]{1,0:T(8,128)(2,1)}, u32[]{:S(2)}) copy-start(bf16[256,256]{1,0:T(8,128)(2,1)} %param.14) | copy-start | bytes 393220
Sparse Core Ops, SparseCore 0:
  276.3 1285.0 reduce-scatter.1
where the time goes:
time: 1580 us; the launch traced here: 1570 us
  waiting for transfers between devices  1290 us (82%)
  blocking collectives  133 us (8%)
  local copies, waits for them, and re-layouts  64.3 us (4%)
  matrix products  51.3 us (3%)
    reduce_scatter x1, waiting for transfers between devices, per_device(): lax.psum_scatter(basis_part, ('wide', 'narrow'), scatter_dimension=0, til...  1150 us
    all_to_all x1, blocking collectives, per_device(): lax.all_to_all(send_feat, 'wide', split_axis=0, concat_axis=0, tiled=True)  101 us
    all_to_all x1, waiting for transfers between devices, per_device(): lax.all_to_all(slot_sums, 'wide', split_axis=0, concat_axis=0, tiled=True)  78 us
    all_to_all x1, waiting for transfers between devices, per_device(): lax.all_to_all(send_cot, 'wide', split_axis=0, concat_axis=0, tiled=True)  63 us
  transfers between devices with their start and end apart: 3, of which 3 were waited for; matrix products, arithmetic and copies ran while one was open for 5% of the time, Pallas kernels for 0%

commit v1 on v0

v1 whole, which is shorter than its diff:
```python
import functools

import jax
import jax.numpy as jnp
from jax import lax
from jax.experimental import pallas as pl
from jax.experimental.pallas import tpu as pltpu
from jax.sharding import PartitionSpec as P

MESH = pl.DeviceIdType.MESH
F32 = jnp.float32
BF16 = jnp.bfloat16
CORES = 2


def layer_kernel(
    nx,
    nz,
    nn,
    meta,
    coef,
    ids_in,
    coef_in,
    feat,
    cot,
    selfw,
    bases_flat,
    bases_split,
    values_hbm,
    out,
    out_basis,
    out_coef,
    ids_v,
    coef_v,
    ids,
    coefs,
    zfeat,
    zcot,
    picked,
    stage,
    ffeat,
    fcot,
    values,
    running,
    slot_g,
    weights,
    self_term,
    rx,
    rb,
    relay,
    grad_acc,
    grad_parts,
    grad_in,
    grad_sum,
    bases_q,
    coef_part,
    coef_recv,
    row_in,
    basis_part,
    basis_in,
    basis_sum,
    basis_rows,
    local_sem,
    id_send,
    id_recv,
    coef_send,
    coef_recv_sem,
    z_send,
    z_recv,
    x_send,
    x_recv,
    ret_send,
    ret_recv,
    relay_recv,
    fwd_send,
    rs_send,
    rs_recv,
    y_send,
    y_recv,
    cp_send,
    cp_recv,
    row_send,
    row_recv,
    zb_send,
    zb_recv,
    xb_send,
    xb_recv,
):
    w = lax.axis_index("wide")
    n = lax.axis_index("narrow")
    x, z, c = w // (CORES * nz), (w // CORES) % nz, w % CORES
    peers = nx * CORES
    owned, block, width = feat.shape
    slots = ffeat.shape[0]
    rels = slot_g.shape[0]
    blocks = values.shape[1]
    nb = basis_part.shape[0] * basis_part.shape[1]
    group = grad_sum.shape[3]
    half = nz // 2
    opposite = 2 * CORES if nx == 4 else peers
    cut = owned // 2

    def slot(xs, zs, cs):
        return (xs * nz + zs) * CORES + cs

    def peer(p):
        return (x + p // CORES) % nx, (c + p % CORES) % CORES

    def row_dev(p):
        xp, cp = peer(p)
        return (slot(xp, z, cp), n)

    def back(p):
        return ((nx - p // CORES) % nx) * CORES + p % CORES

    def z_dev(dz):
        return (slot(x, (z + dz + nz) % nz, c), n)

    def y_dev(dn):
        return (w, (n + dn) % nn)

    def remote(src, dst, ssem, rsem, dev):
        return pltpu.make_async_remote_copy(
            src_ref=src, dst_ref=dst, send_sem=ssem, recv_sem=rsem, device_id=dev, device_id_type=MESH
        )

    def each(lo, hi, body):
        def step(i, carry):
            body(i)
            return carry

        lax.fori_loop(lo, hi, step, 0)

    slot_sums = zfeat

    load_bases = pltpu.make_async_copy(bases_flat, slot_g.at[1], local_sem.at[0])
    load_values = pltpu.make_async_copy(values_hbm, values, local_sem.at[1])
    load_bases_q = pltpu.make_async_copy(bases_split.at[:, :, n], bases_q, local_sem.at[2])
    load_bases.start()
    load_values.start()
    load_bases_q.start()

    barrier = pltpu.get_barrier_semaphore()
    for p in range(1, peers):
        pl.semaphore_signal(barrier, inc=1, device_id=row_dev(p), device_id_type=MESH)
    for dz in range(1, nz):
        pl.semaphore_signal(barrier, inc=1, device_id=z_dev(dz), device_id_type=MESH)
    for dn in range(1, nn):
        pl.semaphore_signal(barrier, inc=1, device_id=y_dev(dn), device_id_type=MESH)
    pl.semaphore_wait(barrier, peers + nz + nn - 3)

    def z_copy(which, own, buf, to, way):
        frm = to - 1 if way > 0 else (to + 1) % nz
        src = own if frm == 0 else buf.at[frm]
        dst = buf.at[to]
        sem = to
        if to == half:
            part = pl.ds(0, cut) if way > 0 else pl.ds(cut, cut)
            src, dst = src.at[part], dst.at[part]
            sem = half if way > 0 else 0
        return remote(src, dst, z_send.at[which, sem], z_recv.at[which, sem], z_dev(way))

    zf = functools.partial(z_copy, 0, feat, zfeat)
    zc = functools.partial(z_copy, 1, cot, zcot)

    def z_first(zcp):
        zcp(1, 1).start()
        zcp(nz - 1, -1).start()

    def z_step(zcp, d):
        if d < half:
            zcp(d, 1).wait_recv()
            zcp(d + 1, 1).start()
            zcp(nz - d, -1).wait_recv()
            zcp(nz - d - 1, -1).start()
        else:
            zcp(half, 1).wait_recv()
            zcp(half, -1).wait_recv()

    def z_done(zcp):
        for d in range(1, half + 1):
            zcp(d, 1).wait_send()
            zcp(nz - d, -1).wait_send()

    def x_copy(which, dst, j, p):
        at = nz if which == 1 and j == 0 else j
        s = slot(x, (z - j + nz) % nz, c)
        return remote(
            stage.at[at, p], dst.at[s], x_send.at[which, j, p], x_recv.at[which, s], row_dev(p)
        )

    def relay_copy(which, j, k):
        p = opposite + k
        if which < 2:
            src, sem = stage.at[nz if which == 1 and j == 0 else j, p], x_send.at[which, j, p]
        else:
            xp, cp = peer(p)
            s = slot(xp, (z - j + nz) % nz, cp)
            src, sem = slot_sums.at[s // owned, s % owned], ret_send.at[j, p]
        by = row_dev(CORES if k == 0 else (nx - 1) * CORES)
        return remote(src, relay.at[which, j, k], sem, relay_recv.at[which, j, k], by)

    def forward_copy(which, j, k):
        to = row_dev(CORES if k == 0 else (nx - 1) * CORES + 1)
        if which < 2:
            s = slot((x + (nx - 1 if k == 0 else 1)) % nx, (z - j + nz) % nz, c)
            dst, sem = (ffeat, fcot)[which].at[s], x_recv.at[which, s]
        else:
            dst, sem = rx.at[j, opposite + k], ret_recv.at[j, opposite + k]
        return remote(relay.at[which, j, k], dst, fwd_send.at[which, j, k], sem, to)

    def forward(which, *chunks):
        if opposite < peers:
            for j in chunks:
                for k in range(CORES):
                    relay_copy(which, j, k).wait_recv()
                    forward_copy(which, j, k).start()

    def x_step(which, own, buf, dst, j):
        src = own
        if j > 0:
            picked[...] = buf[j]
            src = picked
        at = nz if which == 1 and j == 0 else j
        s = slot(x, (z - j + nz) % nz, c)
        if which == 1 and j > 0:
            each(1, peers, lambda p: x_copy(0, ffeat, j, p).wait_send())

        def send(p):
            stage[at, p] = src[ids[p, 0, s]]
            x_copy(which, dst, j, p).start()

        each(1, opposite, send)
        each(opposite + CORES, peers, send)
        if opposite < peers:
            for k in range(CORES):
                stage[at, opposite + k] = src[ids[opposite + k, 0, s]]
                relay_copy(which, j, k).start()
        dst[s] = src[ids[0, 0, s]]

    xf = functools.partial(x_step, 0, feat, zfeat, ffeat)
    xc = functools.partial(x_step, 1, cot, zcot, fcot)

    def x_arrived(which, dst):
        def arrived(q):
            p = q // nz + 1
            xp, cp = peer(p)
            s = slot(xp, q % nz, cp)
            remote(
                stage.at[0, 0], dst.at[s], x_send.at[which, 0, 0], x_recv.at[which, s], row_dev(p)
            ).wait_recv()

        each(0, (peers - 1) * nz, arrived)

    z_first(zf)
    ids_v[0] = ids_in[...]
    coef_v[0] = coef_in[...]

    def small(p):
        return (
            remote(ids_in, ids_v.at[back(p)], id_send.at[p], id_recv.at[back(p)], row_dev(p)),
            remote(coef_in, coef_v.at[back(p)], coef_send.at[p], coef_recv_sem.at[back(p)], row_dev(p)),
        )

    for p in range(1, peers):
        for copy in small(p):
            copy.start()

    load_bases.wait()
    tile = 16
    per = block // tile
    parts = width // block

    def weigh(t):
        hb = t // per
        row = pl.multiple_of((t % per) * tile, tile)
        acc = [jnp.zeros((tile, width), F32) for _ in range(rels)]
        for b in range(nb):
            v = slot_g[1, b * parts + hb, pl.ds(row, tile), :].astype(F32)
            for r in range(rels):
                acc[r] = acc[r] + coef[r * nb + b] * v
        for r in range(rels):
            weights[r, pl.ds(pl.multiple_of(hb * block + row, tile), tile), :] = acc[r].astype(BF16)

    each(0, parts * per, weigh)

    for p in range(1, peers):
        for copy in small(p):
            copy.wait_recv()
    ids_down = pltpu.make_async_copy(ids_v, ids, local_sem.at[3])
    coef_down = pltpu.make_async_copy(coef_v, coefs, local_sem.at[4])
    ids_down.start()
    coef_down.start()
    ids_down.wait()
    coef_down.wait()

    xf(0)
    xc(0)

    def own_term(o):
        self_term[o] = jnp.dot(feat[o], selfw[...], preferred_element_type=F32)

    each(0, owned, own_term)

    for d in range(1, half):
        z_step(zf, d)
        if d == half - 1:
            z_first(zc)
        xf(d)
        xf(nz - d)
        if d == 1:
            forward(0, 0)
            forward(1, 0)
        else:
            forward(0, d - 1, nz - d + 1)
    z_step(zf, half)
    xf(half)
    forward(0, half - 1, nz - half + 1)
    forward(0, half)

    load_values.wait()
    x_arrived(0, ffeat)

    burst = 4

    def messages(r):
        def some(q):
            found = []
            for u in range(burst):
                j = q * burst + u
                found.append(
                    jnp.dot(values[r, j], ffeat[meta[r, j]], preferred_element_type=F32).astype(BF16)
                )
            for u in range(burst):
                j = q * burst + u
                before = meta[rels + r, j]
                earlier = running[jnp.maximum(before, 0)]
                running[j] = jnp.where(before >= 0, earlier, 0.0) + found[u].astype(F32)

        each(0, blocks // burst, some)

        def pick(s):
            at = meta[2 * rels + r, s]
            slot_g[r, s] = jnp.where(at >= 0, running[jnp.maximum(at, 0)], 0.0).astype(BF16)

        each(0, slots, pick)

    messages(0)
    z_step(zc, 1)
    xc(1)
    xc(nz - 1)
    messages(1)
    if half > 2:
        z_step(zc, 2)
        xc(2)
        xc(nz - 2)
    forward(1, 1, nz - 1)

    z_done(zf)

    def sum_slots(m):
        rows = (owned * block, width)
        at = pl.ds(m * owned, owned)
        total = jnp.dot(slot_g[0, at].reshape(rows), weights[0], preferred_element_type=F32)
        for r in range(1, rels):
            total += jnp.dot(slot_g[r, at].reshape(rows), weights[r], preferred_element_type=F32)
        slot_sums[m] = total.astype(BF16).reshape(owned, block, width)

    each(0, nz, sum_slots)

    def ret_copy(j, p):
        xp, cp = peer(p)
        s = slot(xp, (z - j + nz) % nz, cp)
        return remote(
            slot_sums.at[s // owned, s % owned],
            rx.at[j, back(p)],
            ret_send.at[j, p],
            ret_recv.at[j, back(p)],
            row_dev(p),
        )

    def ret_go(*chunks):
        for j in chunks:
            each(1, opposite, lambda p: ret_copy(j, p).start())
            each(opposite + CORES, peers, lambda p: ret_copy(j, p).start())
            if opposite < peers:
                for k in range(CORES):
                    relay_copy(2, j, k).start()

    ret_go(half)
    ret_go(half - 1, half + 1)
    for d in range(3, half):
        z_step(zc, d)
        xc(d)
        xc(nz - d)
        forward(1, d - 1, nz - d + 1)
    if half > 2:
        ret_go(half - 2, half + 2)
    z_step(zc, half)
    xc(half)
    if half > 2:
        forward(1, half - 1, half + 1)
    forward(2, half)
    for d in range(half - 3, 0, -1):
        ret_go(d, nz - d)
    ret_go(0)
    forward(1, half)

    def rs_copy(j, way):
        to = j - 1 if way < 0 else (j + 1) % nz
        at = half if way > 0 and to == 0 else to
        src, dst = ffeat.at[pl.ds(j * owned, owned)], rb.at[at]
        if j == half:
            first = 0 if way < 0 else cut
            src, dst = ffeat.at[pl.ds(j * owned + first, cut)], rb.at[at, pl.ds(first, cut)]
        return remote(src, dst, rs_send.at[at], rs_recv.at[at], z_dev(way))

    def collect(j, o):
        s = slot(x, (z - j + nz) % nz, c)
        total = None
        for p in range(peers):
            weight = jnp.where(ids[p, 0, s] == o, 1.0, 0.0).astype(F32)
            term = (slot_sums[s // owned, s % owned] if p == 0 else rx[j, p]).astype(F32) * weight
            total = term if total is None else total + term
        return total

    def rx_arrived(j):
        each(
            1,
            peers,
            lambda p: remote(
                stage.at[0, 0], rx.at[j, p], ret_send.at[j, 0], ret_recv.at[j, p], row_dev(p)
            ).wait_recv(),
        )

    def reduce_step(j):
        rx_arrived(j)
        lo, hi = 0, 0
        if 0 < j < half:
            rs_copy(j + 1, -1).wait_recv()
            lo, hi = 0, (cut if j + 1 == half else owned)
        elif j > half:
            rs_copy(j - 1, 1).wait_recv()
            lo, hi = (cut if j - 1 == half else 0), owned

        def plain(o):
            ffeat[j * owned + o] = collect(j, o).astype(BF16)

        def more(o):
            ffeat[j * owned + o] = (collect(j, o) + rb[j, o].astype(F32)).astype(BF16)

        if lo > 0:
            each(0, lo, plain)
        if hi > lo:
            each(lo, hi, more)
        if hi < owned:
            each(hi, owned, plain)
        if j <= half:
            rs_copy(j, -1).start()
        if j >= half:
            rs_copy(j, 1).start()

    def reduce_pair(d):
        forward(2, d, nz - d)
        reduce_step(d)
        reduce_step(nz - d)

    reduce_step(half)
    reduce_pair(half - 1)

    x_arrived(1, fcot)

    def relation_grad(r):
        grad_acc[...] = jnp.zeros_like(grad_acc)

        def add(m):
            at = pl.ds(m * owned, owned)
            rows = (owned * block, width)
            grad_acc[...] += lax.dot_general(
                slot_g[r, at].reshape(rows),
                fcot[at].reshape(rows),
                (((0,), (0,)), ((), ())),
                preferred_element_type=F32,
            )

        each(0, nz, add)
        rows = grad_parts.shape[3]
        for h in range(CORES):
            for m in range(nn):
                grad_parts[m, r, h] = grad_acc[pl.ds((h * nn + m) * rows, rows), :]

    relation_grad(0)
    if half > 2:
        reduce_pair(half - 2)
    for r in range(1, rels):
        relation_grad(r)

    def y_copy(dn):
        return remote(
            grad_parts.at[(n + dn) % nn],
            grad_in.at[nn - dn],
            y_send.at[dn],
            y_recv.at[nn - dn],
            y_dev(dn),
        )

    for dn in range(1, nn):
        y_copy(dn).start()

    for d in range(half - 3, 0, -1):
        reduce_pair(d)
    forward(2, 0)

    for dn in range(1, nn):
        y_copy(dn).wait_recv()
    rows = grad_parts.shape[3]
    for r in range(rels):
        for h in range(CORES):
            total = grad_parts[n, r, h]
            for dn in range(1, nn):
                total = total + grad_in[dn, r, h]
            grad_sum[r, h] = total.reshape(nx, group, width)

    def row_copy(p):
        xp, cp = peer(p)
        return remote(
            grad_sum.at[:, cp, xp], row_in.at[back(p)], row_send.at[p], row_recv.at[back(p)], row_dev(p)
        )

    for p in range(1, peers):
        row_copy(p).start()
    row_in[0] = grad_sum[:, c, x]

    load_bases_q.wait()

    def coef_sums(b):
        for r in range(rels):
            total = None
            for h in range(CORES):
                term = (grad_sum[r, h].reshape(rows, width) * bases_q[b, h].astype(F32)).sum(
                    axis=0, keepdims=True
                )
                total = term if total is None else total + term
            line = total[:, :128]
            for k in range(1, width // 128):
                line = line + total[:, k * 128 : (k + 1) * 128]
            coef_part[pl.ds(r * nb + b, 1), :] = line

    each(0, nb, coef_sums)

    def cp_copy(dn):
        return remote(
            coef_part, coef_recv.at[nn - dn], cp_send.at[dn], cp_recv.at[nn - dn], y_dev(dn)
        )

    for dn in range(1, nn):
        cp_copy(dn).start()

    for p in range(1, peers):
        row_copy(p).wait_recv()

    def basis_sums(b):
        total = jnp.zeros((group, width), F32)
        for p in range(peers):
            for r in range(rels):
                total = total + coefs[p, 0, r * nb + b] * row_in[p, r]
        basis_part[b % nz, b // nz] = total

    each(0, nb, basis_sums)

    def zb_copy(dz):
        return remote(
            basis_part.at[(z + dz) % nz],
            basis_in.at[nz - dz],
            zb_send.at[dz],
            zb_recv.at[nz - dz],
            z_dev(dz),
        )

    for dz in range(1, nz):
        zb_copy(dz).start()

    for dz in range(1, nz):
        zb_copy(dz).wait_recv()
    total = basis_part[z]
    for dz in range(1, nz):
        total = total + basis_in[dz]
    basis_sum[...] = total

    def xb_copy(dx):
        return remote(
            basis_sum.at[(x + dx) % nx],
            basis_rows.at[x],
            xb_send.at[dx],
            xb_recv.at[nx - dx],
            row_dev(dx * CORES),
        )

    for dx in range(1, nx):
        xb_copy(dx).start()
    basis_rows[x] = basis_sum[x]

    rx_arrived(0)
    rs_copy(1, -1).wait_recv()
    rs_copy(nz - 1, 1).wait_recv()

    def finish(o):
        arrived = rb[0, o].astype(F32) + rb[half, o].astype(F32)
        out[o] = (self_term[o] + collect(0, o) + arrived).astype(BF16)

    each(0, owned, finish)

    for dx in range(1, nx):
        remote(
            basis_sum.at[0],
            basis_rows.at[(x + dx) % nx],
            xb_send.at[dx],
            xb_recv.at[dx],
            row_dev(dx * CORES),
        ).wait_recv()
    out_basis[...] = basis_rows[...]

    for dn in range(1, nn):
        cp_copy(dn).wait_recv()
    total = coef_part[...]
    for dn in range(1, nn):
        total = total + coef_recv[dn]
    out_coef[...] = total.sum(axis=1, keepdims=True)

    z_done(zc)
    each(1, peers, lambda p: x_copy(0, ffeat, 0, p).wait_send())
    for j in range(nz):
        each(1, peers, lambda p, j=j: x_copy(1, fcot, j, p).wait_send())
        each(1, peers, lambda p, j=j: ret_copy(j, p).wait_send())
        if opposite < peers:
            for which in range(3):
                for k in range(CORES):
                    forward_copy(which, j, k).wait_send()
    for j in range(1, half + 1):
        rs_copy(j, -1).wait_send()
        rs_copy(nz - j, 1).wait_send()
    for p in range(1, peers):
        for copy in small(p):
            copy.wait_send()
        row_copy(p).wait_send()
    for dn in range(1, nn):
        y_copy(dn).wait_send()
        cp_copy(dn).wait_send()
    for dz in range(1, nz):
        zb_copy(dz).wait_send()
    for dx in range(1, nx):
        xb_copy(dx).wait_send()


def per_device(
    nx, nz, nn, features, cotangent, self_weight, bases, basis_coef, block_values, block_slots, fetch_ids
):
    rels, blocks, block, _ = block_values.shape
    width = features.shape[1]
    slots = fetch_ids.shape[0]
    owned = features.shape[0] // block
    nb = bases.shape[0]
    peers = nx * CORES
    rows = width // (CORES * nn)
    group = rows // nx

    row_slot = block_slots[:, :, 0]
    col_slot = block_slots[:, :, 1]
    at = jnp.arange(blocks, dtype=jnp.int32)
    same = (row_slot[:, :, None] == row_slot[:, None, :]) & (at[None, None, :] < at[None, :, None])
    before = jnp.max(jnp.where(same, at[None, None, :], -1), axis=2)
    here = row_slot[:, None, :] == jnp.arange(slots, dtype=jnp.int32)[None, :, None]
    last = jnp.max(jnp.where(here, at[None, None, :], -1), axis=2)
    meta = jnp.concatenate([col_slot, before, last], axis=0)
    coef32 = basis_coef.astype(F32).reshape(rels * nb)
    ids_in = jnp.zeros((1, 128), jnp.int32).at[0, :slots].set(fetch_ids)
    coef_in = jnp.zeros((1, 128), F32).at[0, : rels * nb].set(coef32)

    vmem = pl.BlockSpec(memory_space=pltpu.VMEM)
    smem = pl.BlockSpec(memory_space=pltpu.SMEM)
    anywhere = pl.BlockSpec(memory_space=pl.ANY)
    dma = pltpu.SemaphoreType.DMA
    output, basis_grad, coef_grad = pl.pallas_call(
        functools.partial(layer_kernel, nx, nz, nn),
        out_shape=(
            jax.ShapeDtypeStruct((owned, block, width), BF16),
            jax.ShapeDtypeStruct((nx, group, width), F32),
            jax.ShapeDtypeStruct((rels * nb, 1), F32),
        ),
        in_specs=[smem, smem, vmem, vmem, vmem, vmem, vmem, anywhere, anywhere, anywhere],
        out_specs=(vmem, vmem, vmem),
        scratch_shapes=[
            pltpu.VMEM((peers, 1, 128), jnp.int32),
            pltpu.VMEM((peers, 1, 128), F32),
            pltpu.SMEM((peers, 1, 128), jnp.int32),
            pltpu.SMEM((peers, 1, 128), F32),
            pltpu.VMEM((nz, owned, block, width), BF16),
            pltpu.VMEM((nz, owned, block, width), BF16),
            pltpu.VMEM((owned, block, width), BF16),
            pltpu.VMEM((nz + 1, peers, block, width), BF16),
            pltpu.VMEM((slots, block, width), BF16),
            pltpu.VMEM((slots, block, width), BF16),
            pltpu.VMEM((rels, blocks, block, block), BF16),
            pltpu.VMEM((blocks, block, width), F32),
            pltpu.VMEM((rels, slots, block, width), BF16),
            pltpu.VMEM((rels, width, width), BF16),
            pltpu.VMEM((owned, block, width), F32),
            pltpu.VMEM((nz, peers, block, width), BF16),
            pltpu.VMEM((nz, owned, block, width), BF16),
            pltpu.VMEM((3, nz, CORES, block, width), BF16),
            pltpu.VMEM((width, width), F32),
            pltpu.VMEM((nn, rels, CORES, rows, width), F32),
            pltpu.VMEM((nn, rels, CORES, rows, width), F32),
            pltpu.VMEM((rels, CORES, nx, group, width), F32),
            pltpu.VMEM((nb, CORES, rows, width), BF16),
            pltpu.VMEM((rels * nb, 128), F32),
            pltpu.VMEM((nn, rels * nb, 128), F32),
            pltpu.VMEM((peers, rels, group, width), F32),
            pltpu.VMEM((nz, nx, group, width), F32),
            pltpu.VMEM((nz, nx, group, width), F32),
            pltpu.VMEM((nx, group, width), F32),
            pltpu.VMEM((nx, group, width), F32),
            dma((5,)),
            dma((peers,)),
            dma((peers,)),
            dma((peers,)),
            dma((peers,)),
            dma((2, nz)),
            dma((2, nz)),
            dma((2, nz, peers)),
            dma((2, slots)),
            dma((nz, peers)),
            dma((nz, peers)),
            dma((3, nz, CORES)),
            dma((3, nz, CORES)),
            dma((nz,)),
            dma((nz,)),
            dma((nn,)),
            dma((nn,)),
            dma((nn,)),
            dma((nn,)),
            dma((peers,)),
            dma((peers,)),
            dma((nz,)),
            dma((nz,)),
            dma((nx,)),
            dma((nx,)),
        ],
        compiler_params=pltpu.CompilerParams(
            collective_id=0, has_side_effects=True, vmem_limit_bytes=62 * 1024 * 1024
        ),
    )(
        meta,
        coef32,
        ids_in,
        coef_in,
        features.reshape(owned, block, width),
        cotangent.reshape(owned, block, width),
        self_weight,
        bases.reshape(nb * width // block, block, width),
        bases.reshape(nb, CORES, nn, rows, width),
        block_values,
    )
    return (
        output.reshape(owned * block, width),
        basis_grad.reshape(rows, width),
        coef_grad.reshape(rels, nb),
    )


def solution(mesh, nx=4):
    nz = mesh.shape["wide"] // (CORES * nx)
    return jax.shard_map(
        functools.partial(per_device, nx, nz, mesh.shape["narrow"]),
        mesh=mesh,
        in_specs=(
            P(("wide", "narrow"), None),
            P(("wide", "narrow"), None),
            P(),
            P(),
            P("wide", None),
            P("wide", "narrow", None, None),
            P("wide", "narrow", None),
            P(("wide", "narrow")),
        ),
        out_specs=(P(("wide", "narrow"), None), P(("wide", "narrow"), None), P("wide", None)),
        check_vma=False,
    )
```

time: 1580 us -> 232 us (0.15)
  waiting for transfers between devices: 1290 us -> 0 us
  Pallas kernels: 0 us -> 217 us
  blocking collectives: 133 us -> 0 us
  local copies, waits for them, and re-layouts: 64.3 us -> 7.01 us
  matrix products: 51.3 us -> 0 us
    reduce_scatter x1 -> x0, waiting for transfers between devices: 1150 us -> none  [per_device(): lax.psum_scatter(basis_part, ('wide', 'narrow'), scatter_dimension=0, til...]
    pallas_call x0 -> x1, Pallas kernels: none -> 217 us  [per_device(): pl.pallas_call(functools.partial(layer_kernel, nx, nz, nn), out_shape=(ja...]
    all_to_all x2 -> x0, waiting for transfers between devices: 141 us -> none  [the longest x1 78 us: per_device(): lax.all_to_all(slot_sums, 'wide', split_axis=0, concat_axis=0, tiled=True)]
    all_to_all x2 -> x0, blocking collectives: 123 us -> none  [the longest x1 101 us: per_device(): lax.all_to_all(send_feat, 'wide', split_axis=0, concat_axis=0, tiled=True)]
    dot_general x8 -> x0, matrix products: 51.3 us -> none  [the longest x1 11.7 us: per_device(): jnp.einsum('rkij,rkjd->rkid', block_values, col_feat, preferred_element_t...]
    gather x5 -> x0, local copies, waits for them, and re-layouts: 36 us -> none  [the longest x2 20.7 us: per_device(): col_feat = jnp.take(fetched_feat, col_slot, axis=0)]
    convert_element_type x2 -> x0, local copies, waits for them, and re-layouts: 18.8 us -> none  [the longest x1 12.3 us: per_device(): gathered = jnp.einsum('rkij,rkjd->rkid', block_values, col_feat, preferre...]
  transfers between devices with their start and end apart: 3 -> 0, of which waited for: 3 -> 0; matrix products, arithmetic and copies ran while one was open for 5% -> 0% of each run, Pallas kernels for 0% -> 0%
where the time goes in v1:
time: 232 us; the launch traced here: 229 us
  Pallas kernels  217 us (94%)
  local copies, waits for them, and re-layouts  7.01 us (3%)
  other arithmetic  4.95 us (2%)
    pallas_call x1, Pallas kernels, per_device(): pl.pallas_call(functools.partial(layer_kernel, nx, nz, nn), out_shape=(ja...  217 us

profile of v1, /device:TPU:1, one launch (start us, length us, event | category | flops | bytes accessed | tf_op | source)
XLA Modules:
  0.0 229.2 jit_solution(1860101994208950902)
XLA Ops:
  0.6 0.6 compare_reduce_fusion
  1.3 1.3 fusion
  2.6 0.5 scatter.6.ids_in
  3.1 1.3 broadcast_select_fusion
  4.4 0.1 reshape.118
  4.5 0.5 scatter.9.coef_in
  5.0 1.2 reshape.116.coef
  6.2 0.8 fusion.1
  7.0 0.2 select_reduce_fusion.1
  7.2 0.6 pad_add_fusion.meta
  7.8 216.6 %shard_map.103 = (bf16[8,128,256]{2,1,0:T(8,128)(2,1)}, f32[4,8,256]{2,1,0:T(8,128)}, f32[64,1]{1,0:T(8,128)}) custom-call(s32[6,64]{1,0:T(8,128)} %pad_add_fusion.meta, f32[64]{0:T(128)} %reshape.116.coef, s32[1,128]{1,0:T(1,128)} %scatter.6.ids_in, f32[1,128]{1,0:T(1,128)} %scatter.9.coef_in, bf16[8,128,256]{2,1,0:T(8,128)(2,1)} %bitcast.13, ...), custom_call_target="tpu_custom_call" | custom-call | tf_op jit(solution)/shard_map/pallas_call | solution.py:683
  224.5 0.9 reduce.9
  225.4 0.7 reshape.125
  226.0 1.9 copy.13
  227.9 1.4 copy.14
  (1 shorter events, 0.0 us)

commit v2 on v1

--- a/solution.py
+++ b/solution.py
@@ -17,8 +17,7 @@
     nx,
     nz,
     nn,
-    meta,
-    coef,
+    block_slots,
     ids_in,
     coef_in,
     feat,
@@ -30,8 +29,10 @@
     out,
     out_basis,
     out_coef,
+    meta_v,
     ids_v,
     coef_v,
+    meta,
     ids,
     coefs,
     zfeat,
@@ -47,7 +48,6 @@
     self_term,
     rx,
     rb,
-    relay,
     grad_acc,
     grad_parts,
     grad_in,
@@ -71,8 +71,6 @@
     x_recv,
     ret_send,
     ret_recv,
-    relay_recv,
-    fwd_send,
     rs_send,
     rs_recv,
     y_send,
@@ -97,7 +95,6 @@
     nb = basis_part.shape[0] * basis_part.shape[1]
     group = grad_sum.shape[3]
     half = nz // 2
-    opposite = 2 * CORES if nx == 4 else peers
     cut = owned // 2
 
     def slot(xs, zs, cs):
@@ -130,8 +127,6 @@
             return carry
 
         lax.fori_loop(lo, hi, step, 0)
-
-    slot_sums = zfeat
 
     load_bases = pltpu.make_async_copy(bases_flat, slot_g.at[1], local_sem.at[0])
     load_values = pltpu.make_async_copy(values_hbm, values, local_sem.at[1])
@@ -189,33 +184,6 @@
             stage.at[at, p], dst.at[s], x_send.at[which, j, p], x_recv.at[which, s], row_dev(p)
         )
 
-    def relay_copy(which, j, k):
-        p = opposite + k
-        if which < 2:
-            src, sem = stage.at[nz if which == 1 and j == 0 else j, p], x_send.at[which, j, p]
-        else:
-            xp, cp = peer(p)
-            s = slot(xp, (z - j + nz) % nz, cp)
-            src, sem = slot_sums.at[s // owned, s % owned], ret_send.at[j, p]
-        by = row_dev(CORES if k == 0 else (nx - 1) * CORES)
-        return remote(src, relay.at[which, j, k], sem, relay_recv.at[which, j, k], by)
-
-    def forward_copy(which, j, k):
-        to = row_dev(CORES if k == 0 else (nx - 1) * CORES + 1)
-        if which < 2:
-            s = slot((x + (nx - 1 if k == 0 else 1)) % nx, (z - j + nz) % nz, c)
-            dst, sem = (ffeat, fcot)[which].at[s], x_recv.at[which, s]
-        else:
-            dst, sem = rx.at[j, opposite + k], ret_recv.at[j, opposite + k]
-        return remote(relay.at[which, j, k], dst, fwd_send.at[which, j, k], sem, to)
-
-    def forward(which, *chunks):
-        if opposite < peers:
-            for j in chunks:
-                for k in range(CORES):
-                    relay_copy(which, j, k).wait_recv()
-                    forward_copy(which, j, k).start()
-
     def x_step(which, own, buf, dst, j):
         src = own
         if j > 0:
@@ -230,12 +198,7 @@
             stage[at, p] = src[ids[p, 0, s]]
             x_copy(which, dst, j, p).start()
 
-        each(1, opposite, send)
-        each(opposite + CORES, peers, send)
-        if opposite < peers:
-            for k in range(CORES):
-                stage[at, opposite + k] = src[ids[opposite + k, 0, s]]
-                relay_copy(which, j, k).start()
+        each(1, peers, send)
         dst[s] = src[ids[0, 0, s]]
 
     xf = functools.partial(x_step, 0, feat, zfeat, ffeat)
@@ -253,19 +216,45 @@
         each(0, (peers - 1) * nz, arrived)
 
     z_first(zf)
-    ids_v[0] = ids_in[...]
-    coef_v[0] = coef_in[...]
+    ids_v[0] = jnp.zeros_like(ids_v[0])
+    ids_v[0, :, :slots] = ids_in[...]
+    coef_v[0] = jnp.zeros_like(coef_v[0])
+    coef_v[0, :, :nb] = coef_in[...].astype(F32)
 
     def small(p):
         return (
-            remote(ids_in, ids_v.at[back(p)], id_send.at[p], id_recv.at[back(p)], row_dev(p)),
-            remote(coef_in, coef_v.at[back(p)], coef_send.at[p], coef_recv_sem.at[back(p)], row_dev(p)),
+            remote(ids_v.at[0], ids_v.at[back(p)], id_send.at[p], id_recv.at[back(p)], row_dev(p)),
+            remote(
+                coef_v.at[0], coef_v.at[back(p)], coef_send.at[p], coef_recv_sem.at[back(p)], row_dev(p)
+            ),
         )
 
     for p in range(1, peers):
         for copy in small(p):
             copy.start()
 
+    own_coef_down = pltpu.make_async_copy(coef_v.at[0], coefs.at[0], local_sem.at[4])
+    own_coef_down.start()
+
+    meta_v[...] = jnp.zeros_like(meta_v)
+    down = lax.broadcasted_iota(jnp.int32, (blocks, blocks), 0)
+    across = lax.broadcasted_iota(jnp.int32, (blocks, blocks), 1)
+    down_slot = lax.broadcasted_iota(jnp.int32, (blocks, slots), 0)
+    across_slot = lax.broadcasted_iota(jnp.int32, (blocks, slots), 1)
+    for r in range(rels):
+        row = block_slots[r, 0:1, :]
+        spread = jnp.broadcast_to(row, (blocks, blocks))
+        column = jnp.max(jnp.where(down == across, spread, -1), axis=1, keepdims=True)
+        same = (column == spread) & (down < across)
+        meta_v[r, :, :blocks] = block_slots[r, 1:2, :]
+        meta_v[rels + r, :, :blocks] = jnp.max(jnp.where(same, down, -1), axis=0, keepdims=True)
+        meta_v[2 * rels + r, :, :slots] = jnp.max(
+            jnp.where(column == across_slot, down_slot, -1), axis=0, keepdims=True
+        )
+    meta_down = pltpu.make_async_copy(meta_v, meta, local_sem.at[5])
+    meta_down.start()
+    meta_down.wait()
+    own_coef_down.wait()
     load_bases.wait()
     tile = 16
     per = block // tile
@@ -278,7 +267,7 @@
         for b in range(nb):
             v = slot_g[1, b * parts + hb, pl.ds(row, tile), :].astype(F32)
             for r in range(rels):
-                acc[r] = acc[r] + coef[r * nb + b] * v
+                acc[r] = acc[r] + coefs[0, r, b] * v
         for r in range(rels):
             weights[r, pl.ds(pl.multiple_of(hb * block + row, tile), tile), :] = acc[r].astype(BF16)
 
@@ -288,7 +277,9 @@
         for copy in small(p):
             copy.wait_recv()
     ids_down = pltpu.make_async_copy(ids_v, ids, local_sem.at[3])
-    coef_down = pltpu.make_async_copy(coef_v, coefs, local_sem.at[4])
+    coef_down = pltpu.make_async_copy(
+        coef_v.at[pl.ds(1, peers - 1)], coefs.at[pl.ds(1, peers - 1)], local_sem.at[4]
+    )
     ids_down.start()
     coef_down.start()
     ids_down.wait()
@@ -308,16 +299,12 @@
             z_first(zc)
         xf(d)
         xf(nz - d)
-        if d == 1:
-            forward(0, 0)
-            forward(1, 0)
-        else:
-            forward(0, d - 1, nz - d + 1)
     z_step(zf, half)
     xf(half)
-    forward(0, half - 1, nz - half + 1)
-    forward(0, half)
-
+
+    z_step(zc, 1)
+    xc(1)
+    xc(nz - 1)
     load_values.wait()
     x_arrived(0, ffeat)
 
@@ -329,34 +316,34 @@
             for u in range(burst):
                 j = q * burst + u
                 found.append(
-                    jnp.dot(values[r, j], ffeat[meta[r, j]], preferred_element_type=F32).astype(BF16)
+                    jnp.dot(values[r, j], ffeat[meta[r, 0, j]], preferred_element_type=F32).astype(BF16)
                 )
             for u in range(burst):
                 j = q * burst + u
-                before = meta[rels + r, j]
+                before = meta[rels + r, 0, j]
                 earlier = running[jnp.maximum(before, 0)]
                 running[j] = jnp.where(before >= 0, earlier, 0.0) + found[u].astype(F32)
 
         each(0, blocks // burst, some)
 
         def pick(s):
-            at = meta[2 * rels + r, s]
+            at = meta[2 * rels + r, 0, s]
             slot_g[r, s] = jnp.where(at >= 0, running[jnp.maximum(at, 0)], 0.0).astype(BF16)
 
         each(0, slots, pick)
 
     messages(0)
-    z_step(zc, 1)
-    xc(1)
-    xc(nz - 1)
+    for d in range(2, half - 1):
+        z_step(zc, d)
+        xc(d)
+        xc(nz - d)
     messages(1)
     if half > 2:
-        z_step(zc, 2)
-        xc(2)
-        xc(nz - 2)
-    forward(1, 1, nz - 1)
-
+        z_step(zc, half - 1)
+        xc(half - 1)
+        xc(half + 1)
     z_done(zf)
+    slot_sums = zfeat
 
     def sum_slots(m):
         rows = (owned * block, width)
@@ -379,32 +366,16 @@
             row_dev(p),
         )
 
-    def ret_go(*chunks):
-        for j in chunks:
-            each(1, opposite, lambda p: ret_copy(j, p).start())
-            each(opposite + CORES, peers, lambda p: ret_copy(j, p).start())
-            if opposite < peers:
-                for k in range(CORES):
-                    relay_copy(2, j, k).start()
-
-    ret_go(half)
-    ret_go(half - 1, half + 1)
-    for d in range(3, half):
-        z_step(zc, d)
-        xc(d)
-        xc(nz - d)
-        forward(1, d - 1, nz - d + 1)
-    if half > 2:
-        ret_go(half - 2, half + 2)
+    def ret_go(j):
+        each(1, peers, lambda p: ret_copy(j, p).start())
+
     z_step(zc, half)
     xc(half)
-    if half > 2:
-        forward(1, half - 1, half + 1)
-    forward(2, half)
-    for d in range(half - 3, 0, -1):
-        ret_go(d, nz - d)
+    ret_go(half)
+    for d in range(half - 1, 0, -1):
+        ret_go(d)
+        ret_go(nz - d)
     ret_go(0)
-    forward(1, half)
 
     def rs_copy(j, way):
         to = j - 1 if way < 0 else (j + 1) % nz
@@ -460,14 +431,6 @@
         if j >= half:
             rs_copy(j, 1).start()
 
-    def reduce_pair(d):
-        forward(2, d, nz - d)
-        reduce_step(d)
-        reduce_step(nz - d)
-
-    reduce_step(half)
-    reduce_pair(half - 1)
-
     x_arrived(1, fcot)
 
     def relation_grad(r):
@@ -490,8 +453,7 @@
                 grad_parts[m, r, h] = grad_acc[pl.ds((h * nn + m) * rows, rows), :]
 
     relation_grad(0)
-    if half > 2:
-        reduce_pair(half - 2)
+    reduce_step(half)
     for r in range(1, rels):
         relation_grad(r)
 
@@ -507,9 +469,11 @@
     for dn in range(1, nn):
         y_copy(dn).start()
 
-    for d in range(half - 3, 0, -1):
-        reduce_pair(d)
-    forward(2, 0)
+    def reduce_pair(d):
+        reduce_step(d)
+        reduce_step(nz - d)
+
+    reduce_pair(half - 1)
 
     for dn in range(1, nn):
         y_copy(dn).wait_recv()
@@ -556,6 +520,9 @@
     for dn in range(1, nn):
         cp_copy(dn).start()
 
+    if half > 2:
+        reduce_pair(half - 2)
+
     for p in range(1, peers):
         row_copy(p).wait_recv()
 
@@ -563,7 +530,7 @@
         total = jnp.zeros((group, width), F32)
         for p in range(peers):
             for r in range(rels):
-                total = total + coefs[p, 0, r * nb + b] * row_in[p, r]
+                total = total + coefs[p, r, b] * row_in[p, r]
         basis_part[b % nz, b // nz] = total
 
     each(0, nb, basis_sums)
@@ -579,6 +546,9 @@
 
     for dz in range(1, nz):
         zb_copy(dz).start()
+
+    for d in range(half - 3, 0, -1):
+        reduce_pair(d)
 
     for dz in range(1, nz):
         zb_copy(dz).wait_recv()
@@ -625,17 +595,20 @@
     total = coef_part[...]
     for dn in range(1, nn):
         total = total + coef_recv[dn]
-    out_coef[...] = total.sum(axis=1, keepdims=True)
+    column = total.sum(axis=1, keepdims=True)
+    wide_shape = (rels * nb, rels * nb)
+    diagonal = lax.broadcasted_iota(jnp.int32, wide_shape, 0) == lax.broadcasted_iota(
+        jnp.int32, wide_shape, 1
+    )
+    line = jnp.where(diagonal, jnp.broadcast_to(column, wide_shape), 0.0).sum(axis=0, keepdims=True)
+    for r in range(rels):
+        out_coef[r : r + 1, :] = line[:, r * nb : (r + 1) * nb]
 
     z_done(zc)
     each(1, peers, lambda p: x_copy(0, ffeat, 0, p).wait_send())
     for j in range(nz):
         each(1, peers, lambda p, j=j: x_copy(1, fcot, j, p).wait_send())
         each(1, peers, lambda p, j=j: ret_copy(j, p).wait_send())
-        if opposite < peers:
-            for which in range(3):
-                for k in range(CORES):
-                    forward_copy(which, j, k).wait_send()
     for j in range(1, half + 1):
         rs_copy(j, -1).wait_send()
         rs_copy(nz - j, 1).wait_send()
@@ -652,6 +625,17 @@
         xb_copy(dx).wait_send()
 
 
+def keep_kernel(a, b, c, a_out, b_out, c_out, sem):
+    copies = [
+        pltpu.make_async_copy(src, dst, sem.at[i])
+        for i, (src, dst) in enumerate(((a, a_out), (b, b_out), (c, c_out)))
+    ]
+    for copy in copies:
+        copy.start()
+    for copy in copies:
+        copy.wait()
+
+
 def per_device(
     nx, nz, nn, features, cotangent, self_weight, bases, basis_coef, block_values, block_slots, fetch_ids
 ):
@@ -664,20 +648,7 @@
     rows = width // (CORES * nn)
     group = rows // nx
 
-    row_slot = block_slots[:, :, 0]
-    col_slot = block_slots[:, :, 1]
-    at = jnp.arange(blocks, dtype=jnp.int32)
-    same = (row_slot[:, :, None] == row_slot[:, None, :]) & (at[None, None, :] < at[None, :, None])
-    before = jnp.max(jnp.where(same, at[None, None, :], -1), axis=2)
-    here = row_slot[:, None, :] == jnp.arange(slots, dtype=jnp.int32)[None, :, None]
-    last = jnp.max(jnp.where(here, at[None, None, :], -1), axis=2)
-    meta = jnp.concatenate([col_slot, before, last], axis=0)
-    coef32 = basis_coef.astype(F32).reshape(rels * nb)
-    ids_in = jnp.zeros((1, 128), jnp.int32).at[0, :slots].set(fetch_ids)
-    coef_in = jnp.zeros((1, 128), F32).at[0, : rels * nb].set(coef32)
-
     vmem = pl.BlockSpec(memory_space=pltpu.VMEM)
-    smem = pl.BlockSpec(memory_space=pltpu.SMEM)
     anywhere = pl.BlockSpec(memory_space=pl.ANY)
     dma = pltpu.SemaphoreType.DMA
     output, basis_grad, coef_grad = pl.pallas_call(
@@ -685,15 +656,17 @@
         out_shape=(
             jax.ShapeDtypeStruct((owned, block, width), BF16),
             jax.ShapeDtypeStruct((nx, group, width), F32),
-            jax.ShapeDtypeStruct((rels * nb, 1), F32),
+            jax.ShapeDtypeStruct((rels, nb), F32),
         ),
-        in_specs=[smem, smem, vmem, vmem, vmem, vmem, vmem, anywhere, anywhere, anywhere],
+        in_specs=[vmem, vmem, vmem, vmem, vmem, vmem, anywhere, anywhere, anywhere],
         out_specs=(vmem, vmem, vmem),
         scratch_shapes=[
+            pltpu.VMEM((3 * rels, 1, 128), jnp.int32),
             pltpu.VMEM((peers, 1, 128), jnp.int32),
-            pltpu.VMEM((peers, 1, 128), F32),
+            pltpu.VMEM((peers, rels, 128), F32),
+            pltpu.SMEM((3 * rels, 1, 128), jnp.int32),
             pltpu.SMEM((peers, 1, 128), jnp.int32),
-            pltpu.SMEM((peers, 1, 128), F32),
+            pltpu.SMEM((peers, rels, 128), F32),
             pltpu.VMEM((nz, owned, block, width), BF16),
             pltpu.VMEM((nz, owned, block, width), BF16),
             pltpu.VMEM((owned, block, width), BF16),
@@ -707,7 +680,6 @@
             pltpu.VMEM((owned, block, width), F32),
             pltpu.VMEM((nz, peers, block, width), BF16),
             pltpu.VMEM((nz, owned, block, width), BF16),
-            pltpu.VMEM((3, nz, CORES, block, width), BF16),
             pltpu.VMEM((width, width), F32),
             pltpu.VMEM((nn, rels, CORES, rows, width), F32),
             pltpu.VMEM((nn, rels, CORES, rows, width), F32),
@@ -720,7 +692,7 @@
             pltpu.VMEM((nz, nx, group, width), F32),
             pltpu.VMEM((nx, group, width), F32),
             pltpu.VMEM((nx, group, width), F32),
-            dma((5,)),
+            dma((6,)),
             dma((peers,)),
             dma((peers,)),
             dma((peers,)),
@@ -731,8 +703,6 @@
             dma((2, slots)),
             dma((nz, peers)),
             dma((nz, peers)),
-            dma((3, nz, CORES)),
-            dma((3, nz, CORES)),
             dma((nz,)),
             dma((nz,)),
             dma((nn,)),
@@ -750,10 +720,9 @@
             collective_id=0, has_side_effects=True, vmem_limit_bytes=62 * 1024 * 1024
         ),
     )(
-        meta,
-        coef32,
-        ids_in,
-        coef_in,
+        block_slots.transpose(0, 2, 1),
+        fetch_ids.reshape(1, slots),
+        basis_coef,
         features.reshape(owned, block, width),
         cotangent.reshape(owned, block, width),
         self_weight,
@@ -761,10 +730,18 @@
         bases.reshape(nb, CORES, nn, rows, width),
         block_values,
     )
+    output, basis_grad, coef_grad = pl.pallas_call(
+        keep_kernel,
+        out_shape=tuple(jax.ShapeDtypeStruct(a.shape, a.dtype) for a in (output, basis_grad, coef_grad)),
+        in_specs=[anywhere] * 3,
+        out_specs=(anywhere,) * 3,
+        scratch_shapes=[dma((3,))],
+        compiler_params=pltpu.CompilerParams(vmem_limit_bytes=62 * 1024 * 1024),
+    )(output, basis_grad, coef_grad)
     return (
         output.reshape(owned * block, width),
         basis_grad.reshape(rows, width),
-        coef_grad.reshape(rels, nb),
+        coef_grad,
     )
 
 

time: 232 us -> 200 us (0.86); the launches traced: 229 us -> 200 us
  Pallas kernels: 217 us -> 199 us
  local copies, waits for them, and re-layouts: 7.01 us -> 0 us
  other arithmetic: 4.95 us -> 0 us
    pallas_call x1, Pallas kernels: 217 us -> 181 us  [per_device(): pl.pallas_call(functools.partial(layer_kernel, nx, nz, nn), out_shape=(ja...]
    pallas_call x0 -> x1, Pallas kernels: none -> 18 us  [per_device(): pl.pallas_call(keep_kernel, out_shape=tuple((jax.ShapeDtypeStruct(a.shape...]
    another operation x3 -> x0, other arithmetic: 3.25 us -> none
    unnamed x2 -> x0, local copies, waits for them, and re-layouts: 3.24 us -> none
where the time goes in v2:
time: 200 us
  Pallas kernels  199 us (100%)
    pallas_call x1, Pallas kernels, per_device(): pl.pallas_call(functools.partial(layer_kernel, nx, nz, nn), out_shape=(ja...  181 us
    pallas_call x1, Pallas kernels, per_device(): pl.pallas_call(keep_kernel, out_shape=tuple((jax.ShapeDtypeStruct(a.shape...  18 us

profile of v2, /device:TPU:1, one launch (start us, length us, event | category | flops | bytes accessed | tf_op | source)
XLA Modules:
  0.0 200.0 jit_solution(4203606020193577046)
XLA Ops:
  0.6 181.3 %shard_map.103 = (bf16[8,128,256]{2,1,0:T(8,128)(2,1)}, f32[4,8,256]{2,1,0:T(8,128)}, f32[2,32]{1,0:T(2,128)}) custom-call(s32[2,2,64]{2,1,0:T(2,128)} %bitcast.12, s32[1,64]{1,0:T(1,128)} %bitcast.13, bf16[2,32]{1,0:T(2,128)(2,1)} %coef_in.1, bf16[8,128,256]{2,1,0:T(8,128)(2,1)} %bitcast.10, bf16[8,128,256]{2,1,0:T(8,128)(2,1)} %bitcast.11, ...), custom_call_target="tpu_custom_call" | custom-call | tf_op jit(solution)/shard_map/pallas_call | solution.py:654
  182.0 18.0 %shard_map.104 = (bf16[8,128,256]{2,1,0:T(8,128)(2,1)}, f32[4,8,256]{2,1,0:T(8,128)}, f32[2,32]{1,0:T(2,128)}) custom-call(bf16[8,128,256]{2,1,0:T(8,128)(2,1)} %get-tuple-element.9.a, f32[4,8,256]{2,1,0:T(8,128)} %get-tuple-element.10.b, f32[2,32]{1,0:T(2,128)} %get-tuple-element.11.c), custom_call_target="tpu_custom_call" | custom-call | tf_op jit(solution)/shard_map/pallas_call | solution.py:733

commit v3 on v2

--- a/solution.py
+++ b/solution.py
@@ -255,23 +255,6 @@
     meta_down.start()
     meta_down.wait()
     own_coef_down.wait()
-    load_bases.wait()
-    tile = 16
-    per = block // tile
-    parts = width // block
-
-    def weigh(t):
-        hb = t // per
-        row = pl.multiple_of((t % per) * tile, tile)
-        acc = [jnp.zeros((tile, width), F32) for _ in range(rels)]
-        for b in range(nb):
-            v = slot_g[1, b * parts + hb, pl.ds(row, tile), :].astype(F32)
-            for r in range(rels):
-                acc[r] = acc[r] + coefs[0, r, b] * v
-        for r in range(rels):
-            weights[r, pl.ds(pl.multiple_of(hb * block + row, tile), tile), :] = acc[r].astype(BF16)
-
-    each(0, parts * per, weigh)
 
     for p in range(1, peers):
         for copy in small(p):
@@ -287,6 +270,24 @@
 
     xf(0)
     xc(0)
+
+    load_bases.wait()
+    tile = 16
+    per = block // tile
+    parts = width // block
+
+    def weigh(t):
+        hb = t // per
+        row = pl.multiple_of((t % per) * tile, tile)
+        acc = [jnp.zeros((tile, width), F32) for _ in range(rels)]
+        for b in range(nb):
+            v = slot_g[1, b * parts + hb, pl.ds(row, tile), :].astype(F32)
+            for r in range(rels):
+                acc[r] = acc[r] + coefs[0, r, b] * v
+        for r in range(rels):
+            weights[r, pl.ds(pl.multiple_of(hb * block + row, tile), tile), :] = acc[r].astype(BF16)
+
+    each(0, parts * per, weigh)
 
     def own_term(o):
         self_term[o] = jnp.dot(feat[o], selfw[...], preferred_element_type=F32)
@@ -371,11 +372,15 @@
 
     z_step(zc, half)
     xc(half)
+    def ret_pair(d):
+        if d > 0:
+            ret_go(d)
+            ret_go(nz - d)
+        elif d == 0:
+            ret_go(0)
+
     ret_go(half)
-    for d in range(half - 1, 0, -1):
-        ret_go(d)
-        ret_go(nz - d)
-    ret_go(0)
+    ret_pair(half - 1)
 
     def rs_copy(j, way):
         to = j - 1 if way < 0 else (j + 1) % nz
@@ -454,6 +459,7 @@
 
     relation_grad(0)
     reduce_step(half)
+    ret_pair(half - 2)
     for r in range(1, rels):
         relation_grad(r)
 
@@ -472,6 +478,7 @@
     def reduce_pair(d):
         reduce_step(d)
         reduce_step(nz - d)
+        ret_pair(d - 2)
 
     reduce_pair(half - 1)
 
@@ -625,15 +632,10 @@
         xb_copy(dx).wait_send()
 
 
-def keep_kernel(a, b, c, a_out, b_out, c_out, sem):
-    copies = [
-        pltpu.make_async_copy(src, dst, sem.at[i])
-        for i, (src, dst) in enumerate(((a, a_out), (b, b_out), (c, c_out)))
-    ]
-    for copy in copies:
-        copy.start()
-    for copy in copies:
-        copy.wait()
+def keep_kernel(a, b, c, a_out, b_out, c_out):
+    a_out[...] = a[...]
+    b_out[...] = b[...]
+    c_out[...] = c[...]
 
 
 def per_device(
@@ -733,10 +735,8 @@
     output, basis_grad, coef_grad = pl.pallas_call(
         keep_kernel,
         out_shape=tuple(jax.ShapeDtypeStruct(a.shape, a.dtype) for a in (output, basis_grad, coef_grad)),
-        in_specs=[anywhere] * 3,
-        out_specs=(anywhere,) * 3,
-        scratch_shapes=[dma((3,))],
-        compiler_params=pltpu.CompilerParams(vmem_limit_bytes=62 * 1024 * 1024),
+        in_specs=[vmem] * 3,
+        out_specs=(vmem,) * 3,
     )(output, basis_grad, coef_grad)
     return (
         output.reshape(owned * block, width),

time: 200 us -> 181 us (0.905)
  Pallas kernels: 199 us -> 180 us
    pallas_call x1, Pallas kernels: 18 us -> 1.9 us  [per_device(): pl.pallas_call(keep_kernel, out_shape=tuple((jax.ShapeDtypeStruct(a.shape...]
    pallas_call x1, Pallas kernels: 181 us -> 178 us  [per_device(): pl.pallas_call(functools.partial(layer_kernel, nx, nz, nn), out_shape=(ja...]
where the time goes in v3:
time: 181 us
  Pallas kernels  180 us (99%)
    pallas_call x1, Pallas kernels, per_device(): pl.pallas_call(functools.partial(layer_kernel, nx, nz, nn), out_shape=(ja...  178 us

profile of v3, /device:TPU:1, one launch (start us, length us, event | category | flops | bytes accessed | tf_op | source)
XLA Modules:
  0.0 180.6 jit_solution(3523831164632335988)
XLA Ops:
  0.6 178.1 %shard_map.103 = (bf16[8,128,256]{2,1,0:T(8,128)(2,1)}, f32[4,8,256]{2,1,0:T(8,128)}, f32[2,32]{1,0:T(2,128)}) custom-call(s32[2,2,64]{2,1,0:T(2,128)} %bitcast.12, s32[1,64]{1,0:T(1,128)} %bitcast.13, bf16[2,32]{1,0:T(2,128)(2,1)} %coef_in.1, bf16[8,128,256]{2,1,0:T(8,128)(2,1)} %bitcast.10, bf16[8,128,256]{2,1,0:T(8,128)(2,1)} %bitcast.11, ...), custom_call_target="tpu_custom_call" | custom-call | tf_op jit(solution)/shard_map/pallas_call | solution.py:656
  178.7 1.9 %shard_map.104 = (bf16[8,128,256]{2,1,0:T(8,128)(2,1)}, f32[4,8,256]{2,1,0:T(8,128)}, f32[2,32]{1,0:T(2,128)}) custom-call(bf16[8,128,256]{2,1,0:T(8,128)(2,1)} %get-tuple-element.9.a, f32[4,8,256]{2,1,0:T(8,128)} %get-tuple-element.10.b, f32[2,32]{1,0:T(2,128)} %get-tuple-element.11.c), custom_call_target="tpu_custom_call" | custom-call | tf_op jit(solution)/shard_map/pallas_call | solution.py:735

commit v4 on v3

--- a/solution.py
+++ b/solution.py
@@ -121,6 +121,18 @@
             src_ref=src, dst_ref=dst, send_sem=ssem, recv_sem=rsem, device_id=dev, device_id_type=MESH
         )
 
+    def each_peer(body):
+        if nx == 4:
+
+            def some(i):
+                q = i % 3
+                body((1 + 2 * q - 3 * (q // 2)) * CORES + i // 3)
+
+            each(0, 3 * CORES, some)
+            body(1)
+        else:
+            each(1, peers, body)
+
     def each(lo, hi, body):
         def step(i, carry):
             body(i)
@@ -198,22 +210,21 @@
             stage[at, p] = src[ids[p, 0, s]]
             x_copy(which, dst, j, p).start()
 
-        each(1, peers, send)
+        each_peer(send)
         dst[s] = src[ids[0, 0, s]]
 
     xf = functools.partial(x_step, 0, feat, zfeat, ffeat)
     xc = functools.partial(x_step, 1, cot, zcot, fcot)
 
-    def x_arrived(which, dst):
-        def arrived(q):
-            p = q // nz + 1
+    def x_arrived(which, dst, j):
+        def arrived(p):
             xp, cp = peer(p)
-            s = slot(xp, q % nz, cp)
+            s = slot(xp, (z - j + nz) % nz, cp)
             remote(
                 stage.at[0, 0], dst.at[s], x_send.at[which, 0, 0], x_recv.at[which, s], row_dev(p)
             ).wait_recv()
 
-        each(0, (peers - 1) * nz, arrived)
+        each(1, peers, arrived)
 
     z_first(zf)
     ids_v[0] = jnp.zeros_like(ids_v[0])
@@ -307,7 +318,8 @@
     xc(1)
     xc(nz - 1)
     load_values.wait()
-    x_arrived(0, ffeat)
+    for j in range(nz):
+        x_arrived(0, ffeat, j)
 
     burst = 4
 
@@ -341,8 +353,6 @@
     messages(1)
     if half > 2:
         z_step(zc, half - 1)
-        xc(half - 1)
-        xc(half + 1)
     z_done(zf)
     slot_sums = zfeat
 
@@ -368,10 +378,8 @@
         )
 
     def ret_go(j):
-        each(1, peers, lambda p: ret_copy(j, p).start())
-
-    z_step(zc, half)
-    xc(half)
+        each_peer(lambda p: ret_copy(j, p).start())
+
     def ret_pair(d):
         if d > 0:
             ret_go(d)
@@ -381,6 +389,32 @@
 
     ret_go(half)
     ret_pair(half - 1)
+
+    def grads(*chunks):
+        for j in chunks:
+            x_arrived(1, fcot, j)
+            zo = (z - j + nz) % nz
+
+            def add(r):
+                total = None
+                for xs in range(nx):
+                    at = pl.ds(slot(xs, zo, 0), CORES)
+                    rows = (CORES * block, width)
+                    term = lax.dot_general(
+                        slot_g[r, at].reshape(rows),
+                        fcot[at].reshape(rows),
+                        (((0,), (0,)), ((), ())),
+                        preferred_element_type=F32,
+                    )
+                    total = term if total is None else total + term
+                grad_acc[r] = total if j == 0 else grad_acc[r] + total
+
+            each(0, rels, add)
+
+    if half > 2:
+        grads(0, 1, nz - 1)
+    else:
+        grads(0)
 
     def rs_copy(j, way):
         to = j - 1 if way < 0 else (j + 1) % nz
@@ -436,32 +470,32 @@
         if j >= half:
             rs_copy(j, 1).start()
 
-    x_arrived(1, fcot)
-
-    def relation_grad(r):
-        grad_acc[...] = jnp.zeros_like(grad_acc)
-
-        def add(m):
-            at = pl.ds(m * owned, owned)
-            rows = (owned * block, width)
-            grad_acc[...] += lax.dot_general(
-                slot_g[r, at].reshape(rows),
-                fcot[at].reshape(rows),
-                (((0,), (0,)), ((), ())),
-                preferred_element_type=F32,
-            )
-
-        each(0, nz, add)
-        rows = grad_parts.shape[3]
+    def reduce_pair(d):
+        reduce_step(d)
+        reduce_step(nz - d)
+
+    reduce_step(half)
+    if half > 2:
+        xc(half - 1)
+        xc(half + 1)
+    ret_pair(half - 2)
+    z_step(zc, half)
+    xc(half)
+    for d in range(2, half - 1):
+        grads(d, nz - d)
+    if half > 2:
+        reduce_pair(half - 1)
+        ret_pair(half - 3)
+    grads(half - 1, half + 1)
+    for d in range(half - 2, 1, -1):
+        reduce_pair(d)
+        ret_pair(d - 2)
+    grads(half)
+    rows = grad_parts.shape[3]
+    for r in range(rels):
         for h in range(CORES):
             for m in range(nn):
-                grad_parts[m, r, h] = grad_acc[pl.ds((h * nn + m) * rows, rows), :]
-
-    relation_grad(0)
-    reduce_step(half)
-    ret_pair(half - 2)
-    for r in range(1, rels):
-        relation_grad(r)
+                grad_parts[m, r, h] = grad_acc[r, pl.ds((h * nn + m) * rows, rows), :]
 
     def y_copy(dn):
         return remote(
@@ -475,16 +509,8 @@
     for dn in range(1, nn):
         y_copy(dn).start()
 
-    def reduce_pair(d):
-        reduce_step(d)
-        reduce_step(nz - d)
-        ret_pair(d - 2)
-
-    reduce_pair(half - 1)
-
     for dn in range(1, nn):
         y_copy(dn).wait_recv()
-    rows = grad_parts.shape[3]
     for r in range(rels):
         for h in range(CORES):
             total = grad_parts[n, r, h]
@@ -527,9 +553,6 @@
     for dn in range(1, nn):
         cp_copy(dn).start()
 
-    if half > 2:
-        reduce_pair(half - 2)
-
     for p in range(1, peers):
         row_copy(p).wait_recv()
 
@@ -554,8 +577,7 @@
     for dz in range(1, nz):
         zb_copy(dz).start()
 
-    for d in range(half - 3, 0, -1):
-        reduce_pair(d)
+    reduce_pair(1)
 
     for dz in range(1, nz):
         zb_copy(dz).wait_recv()
@@ -682,7 +704,7 @@
             pltpu.VMEM((owned, block, width), F32),
             pltpu.VMEM((nz, peers, block, width), BF16),
             pltpu.VMEM((nz, owned, block, width), BF16),
-            pltpu.VMEM((width, width), F32),
+            pltpu.VMEM((rels, width, width), F32),
             pltpu.VMEM((nn, rels, CORES, rows, width), F32),
             pltpu.VMEM((nn, rels, CORES, rows, width), F32),
             pltpu.VMEM((rels, CORES, nx, group, width), F32),

time: 181 us -> 186 us (1.028)
  Pallas kernels: 180 us -> 186 us
    pallas_call x1, Pallas kernels: 178 us -> 184 us  [per_device(): pl.pallas_call(functools.partial(layer_kernel, nx, nz, nn), out_shape=(ja...]
where the time goes in v4:
time: 186 us
  Pallas kernels  186 us (100%)
    pallas_call x1, Pallas kernels, per_device(): pl.pallas_call(functools.partial(layer_kernel, nx, nz, nn), out_shape=(ja...  184 us

profile of v4, /device:TPU:1, one launch (start us, length us, event | category | flops | bytes accessed | tf_op | source)
XLA Modules:
  0.0 186.4 jit_solution(12641727319355384693)
XLA Ops:
  0.6 183.8 %shard_map.103 = (bf16[8,128,256]{2,1,0:T(8,128)(2,1)}, f32[4,8,256]{2,1,0:T(8,128)}, f32[2,32]{1,0:T(2,128)}) custom-call(s32[2,2,64]{2,1,0:T(2,128)} %bitcast.12, s32[1,64]{1,0:T(1,128)} %bitcast.13, bf16[2,32]{1,0:T(2,128)(2,1)} %coef_in.1, bf16[8,128,256]{2,1,0:T(8,128)(2,1)} %bitcast.10, bf16[8,128,256]{2,1,0:T(8,128)(2,1)} %bitcast.11, ...), custom_call_target="tpu_custom_call" | custom-call | tf_op jit(solution)/shard_map/pallas_call | solution.py:678
  184.5 1.9 %shard_map.104 = (bf16[8,128,256]{2,1,0:T(8,128)(2,1)}, f32[4,8,256]{2,1,0:T(8,128)}, f32[2,32]{1,0:T(2,128)}) custom-call(bf16[8,128,256]{2,1,0:T(8,128)(2,1)} %get-tuple-element.9.a, f32[4,8,256]{2,1,0:T(8,128)} %get-tuple-element.10.b, f32[2,32]{1,0:T(2,128)} %get-tuple-element.11.c), custom_call_target="tpu_custom_call" | custom-call | tf_op jit(solution)/shard_map/pallas_call | solution.py:757

commit v5 on v3

--- a/solution.py
+++ b/solution.py
@@ -97,21 +97,22 @@
     half = nz // 2
     cut = owned // 2
 
-    def slot(xs, zs, cs):
-        return (xs * nz + zs) * CORES + cs
-
-    def peer(p):
-        return (x + p // CORES) % nx, (c + p % CORES) % CORES
+    zs = [(z + nz - j) % nz for j in range(nz)]
+    along = [
+        ((x + p // CORES) % nx) * (nz * CORES) + (c + p % CORES) % CORES for p in range(peers)
+    ]
+
+    def slot(p, j):
+        return along[p] + zs[j] * CORES
 
     def row_dev(p):
-        xp, cp = peer(p)
-        return (slot(xp, z, cp), n)
+        return (along[p] + z * CORES, n)
 
     def back(p):
         return ((nx - p // CORES) % nx) * CORES + p % CORES
 
     def z_dev(dz):
-        return (slot(x, (z + dz + nz) % nz, c), n)
+        return (along[0] + zs[(nz - dz) % nz] * CORES, n)
 
     def y_dev(dn):
         return (w, (n + dn) % nn)
@@ -120,6 +121,12 @@
         return pltpu.make_async_remote_copy(
             src_ref=src, dst_ref=dst, send_sem=ssem, recv_sem=rsem, device_id=dev, device_id_type=MESH
         )
+
+    def sent(block_ref, sem):
+        remote(block_ref, block_ref, sem, sem, row_dev(1)).wait_send()
+
+    def landed(block_ref, sem):
+        remote(block_ref, block_ref, sem, sem, row_dev(1)).wait_recv()
 
     def each(lo, hi, body):
         def step(i, carry):
@@ -177,12 +184,7 @@
             zcp(d, 1).wait_send()
             zcp(nz - d, -1).wait_send()
 
-    def x_copy(which, dst, j, p):
-        at = nz if which == 1 and j == 0 else j
-        s = slot(x, (z - j + nz) % nz, c)
-        return remote(
-            stage.at[at, p], dst.at[s], x_send.at[which, j, p], x_recv.at[which, s], row_dev(p)
-        )
+    others = pl.ds(1, peers - 1)
 
     def x_step(which, own, buf, dst, j):
         src = own
@@ -190,30 +192,21 @@
             picked[...] = buf[j]
             src = picked
         at = nz if which == 1 and j == 0 else j
-        s = slot(x, (z - j + nz) % nz, c)
+        s = slot(0, j)
         if which == 1 and j > 0:
-            each(1, peers, lambda p: x_copy(0, ffeat, j, p).wait_send())
-
-        def send(p):
+            sent(stage.at[0, others], x_send.at[0, j])
+        for p in range(1, peers):
             stage[at, p] = src[ids[p, 0, s]]
-            x_copy(which, dst, j, p).start()
-
-        each(1, peers, send)
+            remote(
+                stage.at[at, p], dst.at[s], x_send.at[which, j], x_recv.at[which], row_dev(p)
+            ).start()
         dst[s] = src[ids[0, 0, s]]
 
     xf = functools.partial(x_step, 0, feat, zfeat, ffeat)
     xc = functools.partial(x_step, 1, cot, zcot, fcot)
 
     def x_arrived(which, dst):
-        def arrived(q):
-            p = q // nz + 1
-            xp, cp = peer(p)
-            s = slot(xp, q % nz, cp)
-            remote(
-                stage.at[0, 0], dst.at[s], x_send.at[which, 0, 0], x_recv.at[which, s], row_dev(p)
-            ).wait_recv()
-
-        each(0, (peers - 1) * nz, arrived)
+        landed(dst.at[pl.ds(0, (peers - 1) * nz)], x_recv.at[which])
 
     z_first(zf)
     ids_v[0] = jnp.zeros_like(ids_v[0])
@@ -221,17 +214,9 @@
     coef_v[0] = jnp.zeros_like(coef_v[0])
     coef_v[0, :, :nb] = coef_in[...].astype(F32)
 
-    def small(p):
-        return (
-            remote(ids_v.at[0], ids_v.at[back(p)], id_send.at[p], id_recv.at[back(p)], row_dev(p)),
-            remote(
-                coef_v.at[0], coef_v.at[back(p)], coef_send.at[p], coef_recv_sem.at[back(p)], row_dev(p)
-            ),
-        )
-
     for p in range(1, peers):
-        for copy in small(p):
-            copy.start()
+        remote(ids_v.at[0], ids_v.at[back(p)], id_send.at[0], id_recv.at[0], row_dev(p)).start()
+        remote(coef_v.at[0], coef_v.at[back(p)], coef_send.at[0], coef_recv_sem.at[0], row_dev(p)).start()
 
     own_coef_down = pltpu.make_async_copy(coef_v.at[0], coefs.at[0], local_sem.at[4])
     own_coef_down.start()
@@ -256,9 +241,8 @@
     meta_down.wait()
     own_coef_down.wait()
 
-    for p in range(1, peers):
-        for copy in small(p):
-            copy.wait_recv()
+    landed(ids_v.at[others], id_recv.at[0])
+    landed(coef_v.at[others], coef_recv_sem.at[0])
     ids_down = pltpu.make_async_copy(ids_v, ids, local_sem.at[3])
     coef_down = pltpu.make_async_copy(
         coef_v.at[pl.ds(1, peers - 1)], coefs.at[pl.ds(1, peers - 1)], local_sem.at[4]
@@ -356,19 +340,16 @@
 
     each(0, nz, sum_slots)
 
-    def ret_copy(j, p):
-        xp, cp = peer(p)
-        s = slot(xp, (z - j + nz) % nz, cp)
-        return remote(
-            slot_sums.at[s // owned, s % owned],
-            rx.at[j, back(p)],
-            ret_send.at[j, p],
-            ret_recv.at[j, back(p)],
-            row_dev(p),
-        )
-
     def ret_go(j):
-        each(1, peers, lambda p: ret_copy(j, p).start())
+        for p in range(1, peers):
+            s = slot(p, j)
+            remote(
+                slot_sums.at[s // owned, s % owned],
+                rx.at[j, back(p)],
+                ret_send.at[0],
+                ret_recv.at[j],
+                row_dev(p),
+            ).start()
 
     z_step(zc, half)
     xc(half)
@@ -392,7 +373,7 @@
         return remote(src, dst, rs_send.at[at], rs_recv.at[at], z_dev(way))
 
     def collect(j, o):
-        s = slot(x, (z - j + nz) % nz, c)
+        s = slot(0, j)
         total = None
         for p in range(peers):
             weight = jnp.where(ids[p, 0, s] == o, 1.0, 0.0).astype(F32)
@@ -401,13 +382,7 @@
         return total
 
     def rx_arrived(j):
-        each(
-            1,
-            peers,
-            lambda p: remote(
-                stage.at[0, 0], rx.at[j, p], ret_send.at[j, 0], ret_recv.at[j, p], row_dev(p)
-            ).wait_recv(),
-        )
+        landed(rx.at[j, others], ret_recv.at[j])
 
     def reduce_step(j):
         rx_arrived(j)
@@ -467,8 +442,8 @@
         return remote(
             grad_parts.at[(n + dn) % nn],
             grad_in.at[nn - dn],
-            y_send.at[dn],
-            y_recv.at[nn - dn],
+            y_send.at[0],
+            y_recv.at[0],
             y_dev(dn),
         )
 
@@ -482,8 +457,8 @@
 
     reduce_pair(half - 1)
 
-    for dn in range(1, nn):
-        y_copy(dn).wait_recv()
+    if nn > 1:
+        landed(grad_in.at[pl.ds(1, nn - 1)], y_recv.at[0])
     rows = grad_parts.shape[3]
     for r in range(rels):
         for h in range(CORES):
@@ -493,10 +468,8 @@
             grad_sum[r, h] = total.reshape(nx, group, width)
 
     def row_copy(p):
-        xp, cp = peer(p)
-        return remote(
-            grad_sum.at[:, cp, xp], row_in.at[back(p)], row_send.at[p], row_recv.at[back(p)], row_dev(p)
-        )
+        to = grad_sum.at[:, (c + p % CORES) % CORES, (x + p // CORES) % nx]
+        return remote(to, row_in.at[back(p)], row_send.at[0], row_recv.at[0], row_dev(p))
 
     for p in range(1, peers):
         row_copy(p).start()
@@ -521,7 +494,7 @@
 
     def cp_copy(dn):
         return remote(
-            coef_part, coef_recv.at[nn - dn], cp_send.at[dn], cp_recv.at[nn - dn], y_dev(dn)
+            coef_part, coef_recv.at[nn - dn], cp_send.at[0], cp_recv.at[0], y_dev(dn)
         )
 
     for dn in range(1, nn):
@@ -530,8 +503,7 @@
     if half > 2:
         reduce_pair(half - 2)
 
-    for p in range(1, peers):
-        row_copy(p).wait_recv()
+    landed(row_in.at[others], row_recv.at[0])
 
     def basis_sums(b):
         total = jnp.zeros((group, width), F32)
@@ -544,10 +516,10 @@
 
     def zb_copy(dz):
         return remote(
-            basis_part.at[(z + dz) % nz],
+            basis_part.at[zs[nz - dz]],
             basis_in.at[nz - dz],
-            zb_send.at[dz],
-            zb_recv.at[nz - dz],
+            zb_send.at[0],
+            zb_recv.at[0],
             z_dev(dz),
         )
 
@@ -557,8 +529,7 @@
     for d in range(half - 3, 0, -1):
         reduce_pair(d)
 
-    for dz in range(1, nz):
-        zb_copy(dz).wait_recv()
+    landed(basis_in.at[pl.ds(1, nz - 1)], zb_recv.at[0])
     total = basis_part[z]
     for dz in range(1, nz):
         total = total + basis_in[dz]
@@ -568,8 +539,8 @@
         return remote(
             basis_sum.at[(x + dx) % nx],
             basis_rows.at[x],
-            xb_send.at[dx],
-            xb_recv.at[nx - dx],
+            xb_send.at[0],
+            xb_recv.at[0],
             row_dev(dx * CORES),
         )
 
@@ -587,18 +558,11 @@
 
     each(0, owned, finish)
 
-    for dx in range(1, nx):
-        remote(
-            basis_sum.at[0],
-            basis_rows.at[(x + dx) % nx],
-            xb_send.at[dx],
-            xb_recv.at[dx],
-            row_dev(dx * CORES),
-        ).wait_recv()
+    landed(basis_rows.at[pl.ds(0, nx - 1)], xb_recv.at[0])
     out_basis[...] = basis_rows[...]
 
-    for dn in range(1, nn):
-        cp_copy(dn).wait_recv()
+    if nn > 1:
+        landed(coef_recv.at[pl.ds(1, nn - 1)], cp_recv.at[0])
     total = coef_part[...]
     for dn in range(1, nn):
         total = total + coef_recv[dn]
@@ -612,24 +576,21 @@
         out_coef[r : r + 1, :] = line[:, r * nb : (r + 1) * nb]
 
     z_done(zc)
-    each(1, peers, lambda p: x_copy(0, ffeat, 0, p).wait_send())
+    sent(stage.at[0, others], x_send.at[0, 0])
     for j in range(nz):
-        each(1, peers, lambda p, j=j: x_copy(1, fcot, j, p).wait_send())
-        each(1, peers, lambda p, j=j: ret_copy(j, p).wait_send())
+        sent(stage.at[0, others], x_send.at[1, j])
+    sent(rx.at[pl.ds(0, nz), others], ret_send.at[0])
     for j in range(1, half + 1):
         rs_copy(j, -1).wait_send()
         rs_copy(nz - j, 1).wait_send()
-    for p in range(1, peers):
-        for copy in small(p):
-            copy.wait_send()
-        row_copy(p).wait_send()
-    for dn in range(1, nn):
-        y_copy(dn).wait_send()
-        cp_copy(dn).wait_send()
-    for dz in range(1, nz):
-        zb_copy(dz).wait_send()
-    for dx in range(1, nx):
-        xb_copy(dx).wait_send()
+    sent(ids_v.at[others], id_send.at[0])
+    sent(coef_v.at[others], coef_send.at[0])
+    sent(row_in.at[others], row_send.at[0])
+    if nn > 1:
+        sent(grad_in.at[pl.ds(1, nn - 1)], y_send.at[0])
+        sent(coef_recv.at[pl.ds(1, nn - 1)], cp_send.at[0])
+    sent(basis_in.at[pl.ds(1, nz - 1)], zb_send.at[0])
+    sent(basis_sum.at[pl.ds(0, nx - 1)], xb_send.at[0])
 
 
 def keep_kernel(a, b, c, a_out, b_out, c_out):
@@ -695,29 +656,20 @@
             pltpu.VMEM((nx, group, width), F32),
             pltpu.VMEM((nx, group, width), F32),
             dma((6,)),
-            dma((peers,)),
-            dma((peers,)),
-            dma((peers,)),
-            dma((peers,)),
+            dma((1,)),
+            dma((1,)),
+            dma((1,)),
+            dma((1,)),
             dma((2, nz)),
             dma((2, nz)),
-            dma((2, nz, peers)),
-            dma((2, slots)),
-            dma((nz, peers)),
-            dma((nz, peers)),
+            dma((2, nz)),
+            dma((2,)),
+            dma((1,)),
             dma((nz,)),
             dma((nz,)),
-            dma((nn,)),
-            dma((nn,)),
-            dma((nn,)),
-            dma((nn,)),
-            dma((peers,)),
-            dma((peers,)),
             dma((nz,)),
-            dma((nz,)),
-            dma((nx,)),
-            dma((nx,)),
-        ],
+        ]
+        + [dma((1,))] * 10,
         compiler_params=pltpu.CompilerParams(
             collective_id=0, has_side_effects=True, vmem_limit_bytes=62 * 1024 * 1024
         ),

time: 181 us -> 176 us (0.972)
  Pallas kernels: 180 us -> 175 us
    pallas_call x1, Pallas kernels: 178 us -> 173 us  [per_device(): pl.pallas_call(functools.partial(layer_kernel, nx, nz, nn), out_shape=(ja...]
where the time goes in v5:
time: 176 us
  Pallas kernels  175 us (99%)
    pallas_call x1, Pallas kernels, per_device(): pl.pallas_call(functools.partial(layer_kernel, nx, nz, nn), out_shape=(ja...  173 us

profile of v5, /device:TPU:1, one launch (start us, length us, event | category | flops | bytes accessed | tf_op | source)
XLA Modules:
  0.0 176.0 jit_solution(8520340373979973531)
XLA Ops:
  0.6 173.5 %shard_map.103 = (bf16[8,128,256]{2,1,0:T(8,128)(2,1)}, f32[4,8,256]{2,1,0:T(8,128)}, f32[2,32]{1,0:T(2,128)}) custom-call(s32[2,2,64]{2,1,0:T(2,128)} %bitcast.12, s32[1,64]{1,0:T(1,128)} %bitcast.13, bf16[2,32]{1,0:T(2,128)(2,1)} %coef_in.1, bf16[8,128,256]{2,1,0:T(8,128)(2,1)} %bitcast.10, bf16[8,128,256]{2,1,0:T(8,128)(2,1)} %bitcast.11, ...), custom_call_target="tpu_custom_call" | custom-call | tf_op jit(solution)/shard_map/pallas_call | solution.py:617
  174.1 1.9 %shard_map.104 = (bf16[8,128,256]{2,1,0:T(8,128)(2,1)}, f32[4,8,256]{2,1,0:T(8,128)}, f32[2,32]{1,0:T(2,128)}) custom-call(bf16[8,128,256]{2,1,0:T(8,128)(2,1)} %get-tuple-element.9.a, f32[4,8,256]{2,1,0:T(8,128)} %get-tuple-element.10.b, f32[2,32]{1,0:T(2,128)} %get-tuple-element.11.c), custom_call_target="tpu_custom_call" | custom-call | tf_op jit(solution)/shard_map/pallas_call | solution.py:687

commit v6 on v5

--- a/solution.py
+++ b/solution.py
@@ -186,6 +186,9 @@
 
     others = pl.ds(1, peers - 1)
 
+    reach = sorted(range(1, nx), key=lambda dx: min(dx, nx - dx))
+    order = [dx * CORES + k for k in range(CORES) for dx in reach] + list(range(1, CORES))
+
     def x_step(which, own, buf, dst, j):
         src = own
         if j > 0:
@@ -195,7 +198,7 @@
         s = slot(0, j)
         if which == 1 and j > 0:
             sent(stage.at[0, others], x_send.at[0, j])
-        for p in range(1, peers):
+        for p in order:
             stage[at, p] = src[ids[p, 0, s]]
             remote(
                 stage.at[at, p], dst.at[s], x_send.at[which, j], x_recv.at[which], row_dev(p)
@@ -341,7 +344,7 @@
     each(0, nz, sum_slots)
 
     def ret_go(j):
-        for p in range(1, peers):
+        for p in order:
             s = slot(p, j)
             remote(
                 slot_sums.at[s // owned, s % owned],
@@ -411,6 +414,9 @@
         if j >= half:
             rs_copy(j, 1).start()
 
+    reduce_step(half)
+    ret_pair(half - 2)
+
     x_arrived(1, fcot)
 
     def relation_grad(r):
@@ -432,9 +438,14 @@
             for m in range(nn):
                 grad_parts[m, r, h] = grad_acc[pl.ds((h * nn + m) * rows, rows), :]
 
+    def reduce_pair(d):
+        reduce_step(d)
+        reduce_step(nz - d)
+        ret_pair(d - 2)
+
     relation_grad(0)
-    reduce_step(half)
-    ret_pair(half - 2)
+    if half > 2:
+        reduce_pair(half - 1)
     for r in range(1, rels):
         relation_grad(r)
 
@@ -450,12 +461,8 @@
     for dn in range(1, nn):
         y_copy(dn).start()
 
-    def reduce_pair(d):
-        reduce_step(d)
-        reduce_step(nz - d)
-        ret_pair(d - 2)
-
-    reduce_pair(half - 1)
+    if half > 2:
+        reduce_pair(half - 2)
 
     if nn > 1:
         landed(grad_in.at[pl.ds(1, nn - 1)], y_recv.at[0])
@@ -500,9 +507,6 @@
     for dn in range(1, nn):
         cp_copy(dn).start()
 
-    if half > 2:
-        reduce_pair(half - 2)
-
     landed(row_in.at[others], row_recv.at[0])
 
     def basis_sums(b):
@@ -526,7 +530,7 @@
     for dz in range(1, nz):
         zb_copy(dz).start()
 
-    for d in range(half - 3, 0, -1):
+    for d in range(half - 3 if half > 2 else 1, 0, -1):
         reduce_pair(d)
 
     landed(basis_in.at[pl.ds(1, nz - 1)], zb_recv.at[0])
@@ -547,19 +551,6 @@
     for dx in range(1, nx):
         xb_copy(dx).start()
     basis_rows[x] = basis_sum[x]
-
-    rx_arrived(0)
-    rs_copy(1, -1).wait_recv()
-    rs_copy(nz - 1, 1).wait_recv()
-
-    def finish(o):
-        arrived = rb[0, o].astype(F32) + rb[half, o].astype(F32)
-        out[o] = (self_term[o] + collect(0, o) + arrived).astype(BF16)
-
-    each(0, owned, finish)
-
-    landed(basis_rows.at[pl.ds(0, nx - 1)], xb_recv.at[0])
-    out_basis[...] = basis_rows[...]
 
     if nn > 1:
         landed(coef_recv.at[pl.ds(1, nn - 1)], cp_recv.at[0])
@@ -574,6 +565,19 @@
     line = jnp.where(diagonal, jnp.broadcast_to(column, wide_shape), 0.0).sum(axis=0, keepdims=True)
     for r in range(rels):
         out_coef[r : r + 1, :] = line[:, r * nb : (r + 1) * nb]
+
+    rx_arrived(0)
+    rs_copy(1, -1).wait_recv()
+    rs_copy(nz - 1, 1).wait_recv()
+
+    def finish(o):
+        arrived = rb[0, o].astype(F32) + rb[half, o].astype(F32)
+        out[o] = (self_term[o] + collect(0, o) + arrived).astype(BF16)
+
+    each(0, owned, finish)
+
+    landed(basis_rows.at[pl.ds(0, nx - 1)], xb_recv.at[0])
+    out_basis[...] = basis_rows[...]
 
     z_done(zc)
     sent(stage.at[0, others], x_send.at[0, 0])

time: 176 us -> 180 us (1.023)
  Pallas kernels: 175 us -> 179 us
    pallas_call x1, Pallas kernels: 173 us -> 177 us  [per_device(): pl.pallas_call(functools.partial(layer_kernel, nx, nz, nn), out_shape=(ja...]
where the time goes in v6:
time: 180 us
  Pallas kernels  179 us (99%)
    pallas_call x1, Pallas kernels, per_device(): pl.pallas_call(functools.partial(layer_kernel, nx, nz, nn), out_shape=(ja...  177 us

profile of v6, /device:TPU:1, one launch (start us, length us, event | category | flops | bytes accessed | tf_op | source)
XLA Modules:
  0.0 179.6 jit_solution(2501154894615710857)
XLA Ops:
  0.6 177.0 %shard_map.103 = (bf16[8,128,256]{2,1,0:T(8,128)(2,1)}, f32[4,8,256]{2,1,0:T(8,128)}, f32[2,32]{1,0:T(2,128)}) custom-call(s32[2,2,64]{2,1,0:T(2,128)} %bitcast.12, s32[1,64]{1,0:T(1,128)} %bitcast.13, bf16[2,32]{1,0:T(2,128)(2,1)} %coef_in.1, bf16[8,128,256]{2,1,0:T(8,128)(2,1)} %bitcast.10, bf16[8,128,256]{2,1,0:T(8,128)(2,1)} %bitcast.11, ...), custom_call_target="tpu_custom_call" | custom-call | tf_op jit(solution)/shard_map/pallas_call | solution.py:621
  177.7 1.9 %shard_map.104 = (bf16[8,128,256]{2,1,0:T(8,128)(2,1)}, f32[4,8,256]{2,1,0:T(8,128)}, f32[2,32]{1,0:T(2,128)}) custom-call(bf16[8,128,256]{2,1,0:T(8,128)(2,1)} %get-tuple-element.9.a, f32[4,8,256]{2,1,0:T(8,128)} %get-tuple-element.10.b, f32[2,32]{1,0:T(2,128)} %get-tuple-element.11.c), custom_call_target="tpu_custom_call" | custom-call | tf_op jit(solution)/shard_map/pallas_call | solution.py:691

commit v7 on v6

--- a/solution.py
+++ b/solution.py
@@ -186,9 +186,6 @@
 
     others = pl.ds(1, peers - 1)
 
-    reach = sorted(range(1, nx), key=lambda dx: min(dx, nx - dx))
-    order = [dx * CORES + k for k in range(CORES) for dx in reach] + list(range(1, CORES))
-
     def x_step(which, own, buf, dst, j):
         src = own
         if j > 0:
@@ -198,7 +195,7 @@
         s = slot(0, j)
         if which == 1 and j > 0:
             sent(stage.at[0, others], x_send.at[0, j])
-        for p in order:
+        for p in range(1, peers):
             stage[at, p] = src[ids[p, 0, s]]
             remote(
                 stage.at[at, p], dst.at[s], x_send.at[which, j], x_recv.at[which], row_dev(p)
@@ -344,7 +341,7 @@
     each(0, nz, sum_slots)
 
     def ret_go(j):
-        for p in order:
+        for p in range(1, peers):
             s = slot(p, j)
             remote(
                 slot_sums.at[s // owned, s % owned],

time: 180 us -> 179 us (level)
  no operation moved by 1% of the time
where the time goes in v7:
time: 179 us
  Pallas kernels  178 us (99%)
    pallas_call x1, Pallas kernels, per_device(): pl.pallas_call(functools.partial(layer_kernel, nx, nz, nn), out_shape=(ja...  176 us

profile of v7, /device:TPU:1, one launch (start us, length us, event | category | flops | bytes accessed | tf_op | source)
XLA Modules:
  0.0 179.0 jit_solution(16199104637795162650)
XLA Ops:
  0.6 176.5 %shard_map.103 = (bf16[8,128,256]{2,1,0:T(8,128)(2,1)}, f32[4,8,256]{2,1,0:T(8,128)}, f32[2,32]{1,0:T(2,128)}) custom-call(s32[2,2,64]{2,1,0:T(2,128)} %bitcast.12, s32[1,64]{1,0:T(1,128)} %bitcast.13, bf16[2,32]{1,0:T(2,128)(2,1)} %coef_in.1, bf16[8,128,256]{2,1,0:T(8,128)(2,1)} %bitcast.10, bf16[8,128,256]{2,1,0:T(8,128)(2,1)} %bitcast.11, ...), custom_call_target="tpu_custom_call" | custom-call | tf_op jit(solution)/shard_map/pallas_call | solution.py:618
  177.1 1.9 %shard_map.104 = (bf16[8,128,256]{2,1,0:T(8,128)(2,1)}, f32[4,8,256]{2,1,0:T(8,128)}, f32[2,32]{1,0:T(2,128)}) custom-call(bf16[8,128,256]{2,1,0:T(8,128)(2,1)} %get-tuple-element.9.a, f32[4,8,256]{2,1,0:T(8,128)} %get-tuple-element.10.b, f32[2,32]{1,0:T(2,128)} %get-tuple-element.11.c), custom_call_target="tpu_custom_call" | custom-call | tf_op jit(solution)/shard_map/pallas_call | solution.py:688

commit v8 on v5

--- a/solution.py
+++ b/solution.py
@@ -384,8 +384,15 @@
     def rx_arrived(j):
         landed(rx.at[j, others], ret_recv.at[j])
 
-    def reduce_step(j):
+    def gather_sums(j, at):
         rx_arrived(j)
+
+        def one(o):
+            running[at * owned + o] = collect(j, o)
+
+        each(0, owned, one)
+
+    def pass_on(j, at):
         lo, hi = 0, 0
         if 0 < j < half:
             rs_copy(j + 1, -1).wait_recv()
@@ -395,10 +402,10 @@
             lo, hi = (cut if j - 1 == half else 0), owned
 
         def plain(o):
-            ffeat[j * owned + o] = collect(j, o).astype(BF16)
+            ffeat[j * owned + o] = running[at * owned + o].astype(BF16)
 
         def more(o):
-            ffeat[j * owned + o] = (collect(j, o) + rb[j, o].astype(F32)).astype(BF16)
+            ffeat[j * owned + o] = (running[at * owned + o] + rb[j, o].astype(F32)).astype(BF16)
 
         if lo > 0:
             each(0, lo, plain)
@@ -433,7 +440,8 @@
                 grad_parts[m, r, h] = grad_acc[pl.ds((h * nn + m) * rows, rows), :]
 
     relation_grad(0)
-    reduce_step(half)
+    gather_sums(half, 0)
+    pass_on(half, 0)
     ret_pair(half - 2)
     for r in range(1, rels):
         relation_grad(r)
@@ -451,9 +459,11 @@
         y_copy(dn).start()
 
     def reduce_pair(d):
-        reduce_step(d)
-        reduce_step(nz - d)
+        gather_sums(d, 0)
+        gather_sums(nz - d, 1)
         ret_pair(d - 2)
+        pass_on(d, 0)
+        pass_on(nz - d, 1)
 
     reduce_pair(half - 1)
 
@@ -547,19 +557,6 @@
     for dx in range(1, nx):
         xb_copy(dx).start()
     basis_rows[x] = basis_sum[x]
-
-    rx_arrived(0)
-    rs_copy(1, -1).wait_recv()
-    rs_copy(nz - 1, 1).wait_recv()
-
-    def finish(o):
-        arrived = rb[0, o].astype(F32) + rb[half, o].astype(F32)
-        out[o] = (self_term[o] + collect(0, o) + arrived).astype(BF16)
-
-    each(0, owned, finish)
-
-    landed(basis_rows.at[pl.ds(0, nx - 1)], xb_recv.at[0])
-    out_basis[...] = basis_rows[...]
 
     if nn > 1:
         landed(coef_recv.at[pl.ds(1, nn - 1)], cp_recv.at[0])
@@ -574,6 +571,19 @@
     line = jnp.where(diagonal, jnp.broadcast_to(column, wide_shape), 0.0).sum(axis=0, keepdims=True)
     for r in range(rels):
         out_coef[r : r + 1, :] = line[:, r * nb : (r + 1) * nb]
+
+    gather_sums(0, 0)
+    rs_copy(1, -1).wait_recv()
+    rs_copy(nz - 1, 1).wait_recv()
+
+    def finish(o):
+        arrived = rb[0, o].astype(F32) + rb[half, o].astype(F32)
+        out[o] = (self_term[o] + running[o] + arrived).astype(BF16)
+
+    each(0, owned, finish)
+
+    landed(basis_rows.at[pl.ds(0, nx - 1)], xb_recv.at[0])
+    out_basis[...] = basis_rows[...]
 
     z_done(zc)
     sent(stage.at[0, others], x_send.at[0, 0])

time: 176 us -> 175 us (level)
  no operation moved by 1% of the time
where the time goes in v8:
time: 175 us
  Pallas kernels  174 us (99%)
    pallas_call x1, Pallas kernels, per_device(): pl.pallas_call(functools.partial(layer_kernel, nx, nz, nn), out_shape=(ja...  172 us

profile of v8, /device:TPU:1, one launch (start us, length us, event | category | flops | bytes accessed | tf_op | source)
XLA Modules:
  0.0 175.0 jit_solution(6051355548915438672)
XLA Ops:
  0.6 172.4 %shard_map.103 = (bf16[8,128,256]{2,1,0:T(8,128)(2,1)}, f32[4,8,256]{2,1,0:T(8,128)}, f32[2,32]{1,0:T(2,128)}) custom-call(s32[2,2,64]{2,1,0:T(2,128)} %bitcast.12, s32[1,64]{1,0:T(1,128)} %bitcast.13, bf16[2,32]{1,0:T(2,128)(2,1)} %coef_in.1, bf16[8,128,256]{2,1,0:T(8,128)(2,1)} %bitcast.10, bf16[8,128,256]{2,1,0:T(8,128)(2,1)} %bitcast.11, ...), custom_call_target="tpu_custom_call" | custom-call | tf_op jit(solution)/shard_map/pallas_call | solution.py:627
  173.1 1.9 %shard_map.104 = (bf16[8,128,256]{2,1,0:T(8,128)(2,1)}, f32[4,8,256]{2,1,0:T(8,128)}, f32[2,32]{1,0:T(2,128)}) custom-call(bf16[8,128,256]{2,1,0:T(8,128)(2,1)} %get-tuple-element.9.a, f32[4,8,256]{2,1,0:T(8,128)} %get-tuple-element.10.b, f32[2,32]{1,0:T(2,128)} %get-tuple-element.11.c), custom_call_target="tpu_custom_call" | custom-call | tf_op jit(solution)/shard_map/pallas_call | solution.py:697
